TPU v7x, 256 devices: a whole 4x4x8 slice. The times are simulated.
256 devices in a mesh: rows: 4 (over y_lo, core), racks: 8 (over z), pods: 8 (over x, y_hi).
Axes of the slice: x: 4, y: 4 (y_hi: 2, y_lo: 2; y = y_hi * 2 + y_lo), z: 8, core: 2. Of those that a mesh axis runs over, the one named last changes fastest.
Arguments:
- tensor: float32 [8, 16384, 4096], P('rows', 'racks', 'pods'), may hold values from -7372 to 7372, as said below
- factor_b: float32 [16384, 64], P(('racks', 'pods')), may hold values from 0 to 1
- factor_c: float32 [4096, 64], P(('pods', 'racks')), may hold values from 0 to 1
Outputs:
- factor_a: float32 [8, 64], P('rows')
Inputs may be any that keep to these rules, and one draw needn't show every extreme that they name: `tensor`: entries of order one times 0.2 * sqrt(67108864).
All inputs are finite; a program needn't handle non-finite values.
Results may differ from a plain program's by a relative error of at most 0.00013.
Values sent between devices are 32-bit elements; how exact they have to be, the bound alone decides.
No kernel may reach another device: no remote copies, remote signals or barrier semaphores. Data moves between devices by JAX's collectives and lax.ppermute only.
A program may use at most 64 MiB of HBM per device.

v0:
```python
import jax
import jax.numpy as jnp
from jax import lax
from jax.sharding import PartitionSpec as P


def body(tensor, factor_b, factor_c):
    highest = lax.Precision.HIGHEST
    c_block = lax.all_gather(factor_c, "racks", axis=0, tiled=True)
    gram_b_part = jnp.dot(
        factor_b.T, factor_b, precision=highest, preferred_element_type=jnp.float32
    )
    gram_c_part = jnp.dot(
        factor_c.T, factor_c, precision=highest, preferred_element_type=jnp.float32
    )
    mixed = jnp.einsum(
        "ijk,kr->ijr", tensor, c_block, precision=highest, preferred_element_type=jnp.float32
    )
    partial_sum = jnp.sum(
        mixed * lax.all_gather(factor_b, "pods", axis=0, tiled=True)[None], axis=1
    )
    gram_b, gram_c, mttkrp = lax.psum((gram_b_part, gram_c_part, partial_sum), ("racks", "pods"))
    lower = jnp.linalg.cholesky(gram_b * gram_c)
    return jax.scipy.linalg.cho_solve((lower, True), mttkrp.T).T


def solution(mesh):
    in_specs = (P("rows", "racks", "pods"), P(("racks", "pods"), None), P(("pods", "racks"), None))
    out_specs = P("rows", None)
    return jax.shard_map(body, mesh=mesh, in_specs=in_specs, out_specs=out_specs, check_vma=False)
```

profile of v0, /device:TPU:8, one launch (start us, length us, event | category | flops | bytes accessed | tf_op | source)
XLA Modules:
  0.0 445.6 jit_solution(12099255635482629875)
XLA Ops:
  0.0 0.0 copy-start
  0.0 0.0 copy-start.1
  0.0 35.4 %all_gather.7 = f32[2048,64]{0,1:T(8,128)S(1)} all-gather(f32[256,64]{0,1:T(8,128)} %param.4), channel_id=1, replica_groups=mesh['rows'=4,'racks'=8,'pods'=8] {'pods'}, dimensions={0}, use_global_device_ids=true | all-gather | bytes 589824 | tf_op jit(solution)/shard_map/all_gather | solution.py:20
  35.4 28.6 %all_gather.6 = f32[512,64]{1,0:T(8,128)S(1)} all-gather(f32[64,64]{1,0:T(8,128)} %param.5), channel_id=1, replica_groups=mesh['rows'=4,'racks'=8,'pods'=8] {'racks'}, dimensions={0}, use_global_device_ids=true | all-gather | bytes 147456 | tf_op jit(solution)/shard_map/all_gather | solution.py:9
  64.0 10.7 %fusion = f32[2,64]{1,0:T(2,128)S(1)} fusion(f32[2,2048,512]{2,1,0:T(8,128)} %param.3, f32[2048,64]{0,1:T(8,128)S(1)} %all_gather.7, f32[512,64]{1,0:T(8,128)S(1)} %all_gather.6), kind=kOutput, calls=%fused_computation.1 | convolution fusion | flops 1611136896 | bytes 9044480 | tf_op jit(solution)/shard_map/ijk,kr->ijr/dot_general | solution.py:16
  74.7 0.0 copy-done
  74.7 0.2 fusion.8
  74.9 0.0 copy-done.1
  74.9 0.2 fusion.9
  75.2 357.2 %all-reduce = (f32[2,64]{1,0:T(2,128)S(1)}, f32[64,64]{0,1:T(8,128)S(1)}, f32[64,64]{0,1:T(8,128)S(1)}) all-reduce(f32[2,64]{1,0:T(2,128)S(1)} %fusion, f32[64,64]{0,1:T(8,128)S(1)} %fusion.8, f32[64,64]{0,1:T(8,128)S(1)} %fusion.9), channel_id=1, replica_groups=mesh['rows'=4,'racks'=8,'pods'=8] {'racks','pods'}, use_global_device_ids=true, to_apply=%region_5.6 | all-reduce | flops 8320 | bytes 66560 | tf_op jit(solution)/shard_map/psum | solution.py:22
  432.4 0.1 copy.10
  432.5 5.8 %cholesky.16 = f32[64,64]{1,0:T(8,128)S(1)} custom-call(f32[64,64]{1,0:T(8,128)S(1)} %fusion.7), custom_call_target="Cholesky" | custom-call | tf_op jit(solution)/shard_map/jit(cholesky)/cholesky | solution.py:23
  438.4 0.6 compare_reduce_fusion
  439.0 0.7 fusion.2
  439.7 4.9 %custom-call.10 = f32[1,64,64]{1,2,0:T(8,128)S(1)} custom-call(f32[1,64,64]{2,1,0:T(8,128)S(1)} %fusion.2), custom_call_target="InvertDiagBlocksLowerTriangular" | custom-call | tf_op jit(solution)/shard_map/jit(_cho_solve)/triangular_solve | solution.py:24
  444.6 0.3 fusion.5
  444.8 0.8 fusion.3
  (3 shorter events, 0.0 us)
Async XLA Ops:
  0.0 74.7 %copy-start = (f32[256,64]{0,1:T(8,128)S(1)}, f32[256,64]{0,1:T(8,128)}, u32[]{:S(2)}) copy-start(f32[256,64]{0,1:T(8,128)} %param.4) | copy-start | bytes 196612
  0.0 74.9 %copy-start.1 = (f32[64,64]{1,0:T(8,128)S(1)}, f32[64,64]{1,0:T(8,128)}, u32[]{:S(2)}) copy-start(f32[64,64]{1,0:T(8,128)} %param.5) | copy-start | bytes 49156
where the time goes:
time: 446 us
  blocking collectives  421 us (94%)
  matrix products  12.2 us (3%)
  other arithmetic  12.1 us (3%)
    psum x1, blocking collectives, body(): lax.psum((gram_b_part, gram_c_part, partial_sum), ('racks', 'pods'))  357 us
    all_gather x1, blocking collectives, body(): lax.all_gather(factor_b, 'pods', axis=0, tiled=True)[None]  35.4 us
    all_gather x1, blocking collectives, body(): c_block = lax.all_gather(factor_c, 'racks', axis=0, tiled=True)  28.6 us
    dot_general x1, matrix products, body(): jnp.einsum('ijk,kr->ijr', tensor, c_block, precision=highest, preferred_e...  10.7 us

commit v1 on v0

v1 whole, which is shorter than its diff:
```python
import jax
import jax.numpy as jnp
from jax import lax
from jax.sharding import PartitionSpec as P

HIGHEST = lax.Precision.HIGHEST


def share(block, axes, n):
    return lax.all_to_all(jnp.broadcast_to(block[None], (n, *block.shape)), axes, 0, 0, tiled=True)


def body(tensor, factor_b, factor_c):
    racks, pods = lax.axis_size("racks"), lax.axis_size("pods")
    rank = factor_b.shape[1]
    gram_b_own = jnp.dot(factor_b.T, factor_b, precision=HIGHEST)
    first = share(jnp.concatenate([factor_c, gram_b_own], axis=1), "racks", racks)
    c_block = first[:, :, :rank].reshape(-1, rank)
    gram_b_pod = jnp.sum(first[:, :, rank:], axis=0)
    gram_c_own = jnp.dot(c_block.T, c_block, precision=HIGHEST)
    half = factor_b.shape[0] // 2
    second = share(
        jnp.concatenate(
            [
                jnp.concatenate([factor_b[:half], factor_b[half:]], axis=1),
                jnp.concatenate([gram_c_own, gram_b_pod], axis=1),
            ],
            axis=0,
        ),
        "pods",
        pods,
    )
    mixed = jnp.einsum("ijk,kr->ijr", tensor, c_block, precision=HIGHEST)
    b_block = jnp.stack([second[:, :half, :rank], second[:, :half, rank:]], axis=1).reshape(-1, rank)
    partial = jnp.sum(mixed * b_block[None], axis=1)
    everyone = share(partial.reshape(1, -1), ("racks", "pods"), racks * pods)
    grams = jnp.sum(second[:, half:], axis=0)
    lower = jnp.linalg.cholesky(grams[:, :rank] * grams[:, rank:])
    mttkrp = jnp.sum(everyone, axis=0).reshape(-1, rank)
    return jax.scipy.linalg.cho_solve((lower, True), mttkrp.T).T


def solution(mesh):
    in_specs = (P("rows", "racks", "pods"), P(("racks", "pods"), None), P(("pods", "racks"), None))
    out_specs = P("rows", None)
    return jax.shard_map(body, mesh=mesh, in_specs=in_specs, out_specs=out_specs, check_vma=False)
```

time: 446 us -> 80.5 us (0.18)
  blocking collectives: 421 us -> 18.1 us
  waiting for transfers between devices: 0 us -> 17.5 us
  starting transfers between devices: 0 us -> 13.8 us
    psum x1 -> x0, blocking collectives: 357 us -> none  [body(): lax.psum((gram_b_part, gram_c_part, partial_sum), ('racks', 'pods'))]
    all_gather x2 -> x0, blocking collectives: 64 us -> none  [the longest x1 35.4 us: body(): lax.all_gather(factor_b, 'pods', axis=0, tiled=True)[None]]
    all_to_all x0 -> x1, blocking collectives: none -> 18.1 us  [share(): lax.all_to_all(jnp.broadcast_to(block[None], (n, *block.shape)), axes, 0,...]
    all_to_all x0 -> x2, waiting for transfers between devices: none -> 17.5 us  [share(): lax.all_to_all(jnp.broadcast_to(block[None], (n, *block.shape)), axes, 0,...]
    all_to_all x0 -> x2, starting transfers between devices: none -> 13.8 us  [share(): lax.all_to_all(jnp.broadcast_to(block[None], (n, *block.shape)), axes, 0,...]
  transfers between devices with their start and end apart: 0 -> 2, of which waited for: 0 -> 2; matrix products, arithmetic and copies ran while one was open for 0% -> 8% of each run, Pallas kernels for 0% -> 0%
where the time goes in v1:
time: 80.5 us; the launch traced here: 80.1 us
  blocking collectives  18.1 us (22%)
  waiting for transfers between devices  17.5 us (22%)
  starting transfers between devices  13.8 us (17%)
  matrix products  13.4 us (17%)
  other arithmetic  13.3 us (17%)
  local copies, waits for them, and re-layouts  3.93 us (5%)
    all_to_all x1, blocking collectives, share(): lax.all_to_all(jnp.broadcast_to(block[None], (n, *block.shape)), axes, 0,...  18.1 us
    all_to_all x2, waiting for transfers between devices, share(): lax.all_to_all(jnp.broadcast_to(block[None], (n, *block.shape)), axes, 0,...  17.5 us
    all_to_all x2, starting transfers between devices, share(): lax.all_to_all(jnp.broadcast_to(block[None], (n, *block.shape)), axes, 0,...  13.8 us
    dot_general x1, matrix products, body(): mixed = jnp.einsum('ijk,kr->ijr', tensor, c_block, precision=HIGHEST)  10.8 us
    another operation x3, other arithmetic, body(): lower = jnp.linalg.cholesky(grams[:, :rank] * grams[:, rank:])  6.52 us
    another operation x2, other arithmetic, body(): return jax.scipy.linalg.cho_solve((lower, True), mttkrp.T).T  5.55 us
  transfers between devices with their start and end apart: 2, of which 2 were waited for; matrix products, arithmetic and copies ran while one was open for 8% of the time, Pallas kernels for 0%

profile of v1, /device:TPU:8, one launch (start us, length us, event | category | flops | bytes accessed | tf_op | source)
XLA Modules:
  0.0 80.1 jit_solution(11484945604985891884)
XLA Ops:
  0.0 1.1 %fusion.11 = f32[64,64]{1,0:T(8,128)S(1)} fusion(f32[256,64]{0,1:T(8,128)} %param.4), kind=kOutput, calls=%fused_computation.27 | convolution fusion | flops 12582912 | bytes 81920 | tf_op jit(solution)/shard_map/dot_general | solution.py:16
  1.1 0.8 %pad_maximum_fusion.2 = f32[64,128]{1,0:T(8,128)S(1)} fusion(f32[64,64]{1,0:T(8,128)S(1)} %fusion.11, f32[64,64]{1,0:T(8,128)} %param.5), kind=kLoop, calls=%fused_computation.12 | loop fusion | flops 8192 | bytes 65536 | tf_op jit(solution)/shard_map/concatenate | solution.py:17
  2.0 0.7 broadcast_in_dim.9
  2.7 8.5 %all-to-all-start = ((f32[8,64,128]{2,1,0:T(8,128)}), f32[8,64,128]{2,1,0:T(8,128)S(1)}, u32[]{:S(2)}, u32[]{:S(2)}) async-start(f32[8,64,128]{2,1,0:T(8,128)} %broadcast_in_dim.9), calls=%async_computation | async-start | bytes 524288 | tf_op jit(solution)/shard_map/all_to_all | solution.py:10
  11.1 0.8 fusion.9
  11.9 11.1 %all-to-all-done = f32[8,64,128]{2,1,0:T(8,128)S(1)} async-done(((f32[8,64,128]{2,1,0:T(8,128)}), f32[8,64,128]{2,1,0:T(8,128)S(1)}, u32[]{:S(2)}, u32[]{:S(2)}) %all-to-all-start) | async-done | bytes 262176 | tf_op jit(solution)/shard_map/all_to_all | solution.py:10
  23.0 0.6 convolution_bitcast_fusion.1
  23.6 0.1 slice_reduce_fusion.1
  23.8 0.1 pad_maximum_fusion.3
  23.8 0.1 copy.37
  24.0 0.1 copy.38
  24.0 0.1 broadcast_in_dim.10
  24.1 18.1 %all_to_all.15 = f32[8,192,128]{2,1,0:T(8,128)S(1)} all-to-all(f32[8,192,128]{2,1,0:T(8,128)S(1)} %broadcast_in_dim.10), channel_id=1, replica_groups=mesh['rows'=4,'racks'=8,'pods'=8] {'pods'}, dimensions={0} | all-to-all | bytes 1572864 | tf_op jit(solution)/shard_map/all_to_all | solution.py:10
  42.2 0.1 fusion.10
  42.3 0.1 copy.49
  42.4 0.1 copy.48
  42.5 0.1 copy.41
  42.6 5.8 %cholesky.16 = f32[64,64]{1,0:T(8,128)S(1)} custom-call(f32[64,64]{1,0:T(8,128)S(1)} %fusion.7), custom_call_target="Cholesky" | custom-call | tf_op jit(solution)/shard_map/jit(cholesky)/cholesky | solution.py:38
  48.5 0.6 compare_reduce_fusion
  49.1 0.2 slice_bitcast_fusion.1
  49.3 0.1 pad_maximum_fusion
  49.4 0.5 copy.43
  49.9 0.4 mul.14
  50.3 10.8 %fusion.1 = f32[2,64]{1,0:T(2,128)S(1)} fusion(f32[512,64,1]{1,0,2:T(8,128)S(1)} %bitcast.35, f32[2,2048,512]{2,1,0:T(8,128)} %param.3, f32[2048,64]{0,1:T(8,128)S(1)} %mul.14), kind=kOutput, calls=%fused_computation.2 | convolution fusion | flops 1611136896 | bytes 9044480 | tf_op jit(solution)/shard_map/ijk,kr->ijr/dot_general | solution.py:33
  61.1 0.1 broadcast_in_dim.11
  61.2 0.6 broadcast_in_dim.24
  61.8 5.3 %all-to-all-start.2 = ((f32[64,1,128]{2,1,0:T(1,128)}), f32[64,1,128]{2,1,0:T(1,128)S(1)}, u32[]{:S(2)}, u32[]{:S(2)}) async-start(f32[64,1,128]{2,1,0:T(1,128)} %broadcast_in_dim.24), calls=%async_computation.2 | async-start | bytes 65536 | tf_op jit(solution)/shard_map/all_to_all | solution.py:10
  67.1 0.7 fusion.2
  67.8 4.9 %custom-call.10 = f32[1,64,64]{1,2,0:T(8,128)S(1)} custom-call(f32[1,64,64]{2,1,0:T(8,128)S(1)} %fusion.2), custom_call_target="InvertDiagBlocksLowerTriangular" | custom-call | tf_op jit(solution)/shard_map/jit(_cho_solve)/triangular_solve | solution.py:40
  72.7 6.4 %all-to-all-done.2 = f32[64,1,128]{2,1,0:T(1,128)S(1)} async-done(((f32[64,1,128]{2,1,0:T(1,128)}), f32[64,1,128]{2,1,0:T(1,128)S(1)}, u32[]{:S(2)}, u32[]{:S(2)}) %all-to-all-start.2) | async-done | bytes 32800 | tf_op jit(solution)/shard_map/all_to_all | solution.py:10
  79.1 0.1 reshape.28
  79.2 0.1 fusion.5
  79.3 0.7 fusion.3
  (6 shorter events, 0.1 us)
Async XLA Ops:
  2.7 20.3 %all-to-all-start = ((f32[8,64,128]{2,1,0:T(8,128)}), f32[8,64,128]{2,1,0:T(8,128)S(1)}, u32[]{:S(2)}, u32[]{:S(2)}) async-start(f32[8,64,128]{2,1,0:T(8,128)} %broadcast_in_dim.9), calls=%async_computation | async-start | bytes 524288 | tf_op jit(solution)/shard_map/all_to_all | solution.py:10
  61.8 17.3 %all-to-all-start.2 = ((f32[64,1,128]{2,1,0:T(1,128)}), f32[64,1,128]{2,1,0:T(1,128)S(1)}, u32[]{:S(2)}, u32[]{:S(2)}) async-start(f32[64,1,128]{2,1,0:T(1,128)} %broadcast_in_dim.24), calls=%async_computation.2 | async-start | bytes 65536 | tf_op jit(solution)/shard_map/all_to_all | solution.py:10

commit v2 on v0

v2 whole, which is shorter than its diff:
```python
import jax
import jax.numpy as jnp
from jax import lax
from jax.experimental import pallas as pl
from jax.experimental.pallas import tpu as pltpu
from jax.sharding import PartitionSpec as P

F32, BF16 = jnp.float32, jnp.bfloat16
VMEM = pl.BlockSpec(memory_space=pltpu.VMEM)
LIMIT = 40 * 1024 * 1024
ROWS = 512


def pieces(x, n):
    out = []
    for _ in range(n - 1):
        out.append(x.astype(BF16))
        x = x - out[-1].astype(F32)
    return out + [x.astype(BF16)]


def gram(x, dim):
    parts = pieces(x, 3)
    return sum(
        lax.dot_general(a, b, (((dim,), (dim,)), ((), ())), preferred_element_type=F32)
        for n, a in enumerate(parts)
        for b in parts[: 3 - n]
    )


def first_kernel(bt_ref, c_ref, out_ref):
    block = jnp.concatenate([c_ref[...], gram(bt_ref[...], 1)], axis=1)
    for n in range(out_ref.shape[0]):
        out_ref[n] = block


def second_kernel(bt_ref, in_ref, out_ref, w_ref):
    devices, rows, _ = in_ref.shape
    rank = bt_ref.shape[0]
    block = in_ref[...].reshape(devices * rows, 2 * rank)
    c = block[:, :rank]
    gram_b = jnp.sum(in_ref[...], axis=0)[:, rank:]
    grams = jnp.concatenate([gram(c, 0), gram_b], axis=1)
    half = bt_ref.shape[1] // 2
    b = jnp.concatenate([bt_ref[:, :half].T, bt_ref[:, half:].T], axis=1)
    for n in range(out_ref.shape[0]):
        out_ref[n, :half] = b
        out_ref[n, half:] = grams
    w_ref[...] = jnp.concatenate(pieces(c, 2), axis=1)


def mixed_kernel(t_ref, w_ref, out_ref):
    high, low = pieces(t_ref[0], 2)
    w = w_ref[...]
    both = jnp.dot(high, w, preferred_element_type=F32) + jnp.dot(low, w, preferred_element_type=F32)
    rank = w.shape[1] // 2
    both = both + pltpu.roll(both, rank, 1)
    left = lax.broadcasted_iota(jnp.int32, out_ref.shape[2:], 1) < rank
    half = out_ref.shape[2]
    for n in range(out_ref.shape[1]):
        at = 2 * half * n
        out_ref[0, n] = jnp.where(left, both[at : at + half], both[at + half : at + 2 * half])


def partial_kernel(mixed_ref, in_ref, out_ref):
    half = mixed_ref.shape[2]
    width = mixed_ref.shape[3]
    rows = []
    for i in range(2):
        total = jnp.zeros((8, width), F32)
        for n in range(mixed_ref.shape[1]):
            product = mixed_ref[i, n] * in_ref[n, :half]
            total = total + jnp.sum(product.reshape(half // 8, 8, width), axis=0)
        row = jnp.sum(total, axis=0, keepdims=True)
        rows.append(row + pltpu.roll(row, width // 2, 1))
    left = lax.broadcasted_iota(jnp.int32, (1, width), 1) < width // 2
    out_ref[...] = jnp.broadcast_to(jnp.where(left, rows[0], rows[1])[None], out_ref.shape)


def factor_kernel(in_ref, out_ref):
    rank = in_ref.shape[1] // 3
    grams = jnp.sum(in_ref[:, 2 * rank :], axis=0)
    a = grams[:, :rank] * grams[:, rank:]
    eye = lax.broadcasted_iota(jnp.int32, (rank, rank), 0) == lax.broadcasted_iota(jnp.int32, (rank, rank), 1)
    a = jnp.concatenate([a, eye.astype(F32)], axis=1)
    row_at = lax.broadcasted_iota(jnp.int32, a.shape, 0)
    for k in range(rank):
        row = a[k : k + 1]
        column = a[:, k : k + 1]
        scale = lax.rsqrt(row[:, k : k + 1])
        row = row * scale
        out_ref[k : k + 1] = row[:, rank:]
        a = jnp.where(row_at > k, a - (column * scale) * row, a)


def last_kernel(in_ref, inverse_ref, out_ref):
    rank = inverse_ref.shape[0]
    total = jnp.sum(in_ref[:, 0, :], axis=0, keepdims=True)
    x = jnp.concatenate([total[:, :rank], total[:, rank:]], axis=0)
    inverse = inverse_ref[...]
    x = lax.dot_general(x, inverse, (((1,), (1,)), ((), ())), precision=lax.Precision.HIGHEST, preferred_element_type=F32)
    out_ref[...] = jnp.dot(x, inverse, precision=lax.Precision.HIGHEST, preferred_element_type=F32)


def call(kernel, name, ins, outs, **more):
    many = isinstance(outs, list)
    return pl.pallas_call(
        kernel,
        name=name,
        in_specs=[VMEM] * ins,
        out_specs=[VMEM] * len(outs) if many else VMEM,
        out_shape=outs,
        compiler_params=pltpu.CompilerParams(vmem_limit_bytes=LIMIT),
        **more,
    )


def exchange(x, axes):
    return lax.all_to_all(x, axes, 0, 0, tiled=True)


def body(tensor, factor_b, factor_c):
    racks, pods = lax.axis_size("racks"), lax.axis_size("pods")
    slabs, extent_j, extent_k = tensor.shape
    own_b, rank = factor_b.shape
    own_c = factor_c.shape[0]
    half, width = own_b // 2, 2 * rank
    shape = jax.ShapeDtypeStruct
    bt = factor_b.T

    first = call(first_kernel, "first", 2, shape((racks, own_c, width), F32))(bt, factor_c)
    first = exchange(first, "racks")
    second, w = call(
        second_kernel, "second", 2, [shape((pods, half + rank, width), F32), shape((extent_k, width), BF16)]
    )(bt, first)
    second = exchange(second, "pods")
    chunks = ROWS // own_b
    mixed = pl.pallas_call(
        mixed_kernel,
        name="mixed",
        grid=(slabs, extent_j // ROWS),
        in_specs=[
            pl.BlockSpec((1, ROWS, extent_k), lambda i, j: (i, j, 0)),
            pl.BlockSpec((extent_k, width), lambda i, j: (0, 0)),
        ],
        out_specs=pl.BlockSpec((1, chunks, half, width), lambda i, j: (i, j, 0, 0)),
        out_shape=shape((slabs, pods, half, width), F32),
        compiler_params=pltpu.CompilerParams(vmem_limit_bytes=LIMIT),
        cost_estimate=pl.CostEstimate(
            flops=4 * tensor.size * width, bytes_accessed=4 * tensor.size, transcendentals=0
        ),
    )(tensor, w)
    partial = call(partial_kernel, "partial", 2, shape((racks * pods, 1, width), F32))(mixed, second)
    everyone = exchange(partial, ("racks", "pods"))
    inverse = call(
        factor_kernel,
        "factor",
        1,
        shape((rank, rank), F32),
        cost_estimate=pl.CostEstimate(flops=4_000_000_000, bytes_accessed=800_000, transcendentals=64),
    )(second)
    return call(last_kernel, "last", 2, shape((slabs, rank), F32))(everyone, inverse)


def solution(mesh):
    in_specs = (P("rows", "racks", "pods"), P(("racks", "pods"), None), P(("pods", "racks"), None))
    out_specs = P("rows", None)
    return jax.shard_map(body, mesh=mesh, in_specs=in_specs, out_specs=out_specs, check_vma=False)
```

time: 446 us -> 61 us (0.14)
  blocking collectives: 421 us -> 20.1 us
  Pallas kernels: 0 us -> 13 us
  matrix products: 12.2 us -> 0 us
  other arithmetic: 12.1 us -> 0 us
  starting transfers between devices: 0 us -> 11.7 us
  waiting for transfers between devices: 0 us -> 10.8 us
  local copies, waits for them, and re-layouts: 0.08 us -> 4.97 us
    psum x1 -> x0, blocking collectives: 357 us -> none  [body(): lax.psum((gram_b_part, gram_c_part, partial_sum), ('racks', 'pods'))]
    all_gather x2 -> x0, blocking collectives: 64 us -> none  [the longest x1 35.4 us: body(): lax.all_gather(factor_b, 'pods', axis=0, tiled=True)[None]]
    all_to_all x0 -> x1, blocking collectives: none -> 20.1 us  [exchange(): return lax.all_to_all(x, axes, 0, 0, tiled=True)]
    pallas_call x0 -> x6, Pallas kernels: none -> 13 us  [the longest x1 5.45 us: body(): call(factor_kernel, 'factor', 1, shape((rank, rank), F32), cost_estimate=...]
    another operation x5 -> x0, other arithmetic: 12.1 us -> none  [the longest x3 6.52 us: body(): lower = jnp.linalg.cholesky(gram_b * gram_c)]
    all_to_all x0 -> x2, starting transfers between devices: none -> 11.7 us  [exchange(): return lax.all_to_all(x, axes, 0, 0, tiled=True)]
    dot_general x3 -> x0, matrix products: 11.1 us -> none  [the longest x1 10.7 us: body(): jnp.einsum('ijk,kr->ijr', tensor, c_block, precision=highest, preferred_e...]
    all_to_all x0 -> x2, waiting for transfers between devices: none -> 10.8 us  [exchange(): return lax.all_to_all(x, axes, 0, 0, tiled=True)]
  transfers between devices with their start and end apart: 0 -> 2, of which waited for: 0 -> 2; matrix products, arithmetic and copies ran while one was open for 0% -> 0% of each run, Pallas kernels for 0% -> 16%
where the time goes in v2:
time: 61 us; the launch traced here: 60.6 us
  blocking collectives  20.1 us (33%)
  Pallas kernels  13 us (21%)
  starting transfers between devices  11.7 us (19%)
  waiting for transfers between devices  10.8 us (18%)
  local copies, waits for them, and re-layouts  4.97 us (8%)
    all_to_all x1, blocking collectives, exchange(): return lax.all_to_all(x, axes, 0, 0, tiled=True)  20.1 us
    all_to_all x2, starting transfers between devices, exchange(): return lax.all_to_all(x, axes, 0, 0, tiled=True)  11.7 us
    all_to_all x2, waiting for transfers between devices, exchange(): return lax.all_to_all(x, axes, 0, 0, tiled=True)  10.8 us
    pallas_call x1, Pallas kernels, body(): call(factor_kernel, 'factor', 1, shape((rank, rank), F32), cost_estimate=...  5.45 us
    unnamed x6, local copies, waits for them, and re-layouts  4.97 us
    pallas_call x1, Pallas kernels, body(): pl.pallas_call(mixed_kernel, name='mixed', grid=(slabs, extent_j // ROWS)...  4.21 us
    pallas_call x1, Pallas kernels, body(): call(second_kernel, 'second', 2, [shape((pods, half + rank, width), F32),...  1.23 us
  transfers between devices with their start and end apart: 2, of which 2 were waited for; matrix products, arithmetic and copies ran while one was open for 0% of the time, Pallas kernels for 16%

profile of v2, /device:TPU:8, one launch (start us, length us, event | category | flops | bytes accessed | tf_op | source)
XLA Modules:
  0.0 60.6 jit_solution(4723102667004273159)
XLA Ops:
  0.0 0.0 copy-start.1
  0.0 0.8 %copy-done.1 = f32[256,64]{0,1:T(8,128)S(1)} copy-done((f32[256,64]{0,1:T(8,128)S(1)}, f32[256,64]{0,1:T(8,128)}, u32[]{:S(2)}) %copy-start.1) | copy-done | bytes 65560
  0.8 0.0 copy-start.2
  0.8 0.8 %copy-done.2 = f32[64,64]{1,0:T(8,128)S(1)} copy-done((f32[64,64]{1,0:T(8,128)S(1)}, f32[64,64]{1,0:T(8,128)}, u32[]{:S(2)}) %copy-start.2) | copy-done | bytes 16408
  1.6 0.3 first.1
  1.9 20.1 %all_to_all.15.in_ref = f32[8,64,128]{2,1,0:T(8,128)S(1)} all-to-all(f32[8,64,128]{2,1,0:T(8,128)S(1)} %first.1), channel_id=1, replica_groups=mesh['rows'=4,'racks'=8,'pods'=8] {'racks'}, dimensions={0} | all-to-all | bytes 524288 | tf_op jit(solution)/shard_map/all_to_all | solution.py:119
  22.0 1.2 %second.1 = (f32[8,192,128]{2,1,0:T(8,128)}, bf16[512,128]{1,0:T(8,128)(2,1)S(1)}) custom-call(f32[64,256]{1,0:T(8,128)S(1)} %bitcast.2, f32[8,64,128]{2,1,0:T(8,128)S(1)} %all_to_all.15.in_ref), custom_call_target="tpu_custom_call" | custom-call | tf_op jit(solution)/shard_map/second/pallas_call | solution.py:133
  23.3 6.0 %all-to-all-start.1 = ((f32[8,192,128]{2,1,0:T(8,128)}), f32[8,192,128]{2,1,0:T(8,128)S(1)}, u32[]{:S(2)}, u32[]{:S(2)}) async-start(f32[8,192,128]{2,1,0:T(8,128)} %get-tuple-element.8), calls=%async_computation.1 | async-start | bytes 1572864 | tf_op jit(solution)/shard_map/all_to_all | solution.py:119
  29.3 0.0 copy-start
  29.3 3.4 %copy-done = f32[2,2048,512]{2,1,0:T(8,128)S(1)} copy-done((f32[2,2048,512]{2,1,0:T(8,128)S(1)}, f32[2,2048,512]{2,1,0:T(8,128)}, u32[]{:S(2)}) %copy-start) | copy-done | bytes 8388632
  32.7 4.2 %mixed.1.mixed_ref = f32[2,8,128,128]{3,2,1,0:T(8,128)S(1)} custom-call(f32[2,2048,512]{2,1,0:T(8,128)S(1)} %copy-done, bf16[512,128]{1,0:T(8,128)(2,1)S(1)} %get-tuple-element.7.w_ref), custom_call_target="tpu_custom_call" | custom-call | flops 1073741824 | bytes 8388608 | tf_op jit(solution)/shard_map/mixed/pallas_call | solution.py:138
  36.9 4.4 %all-to-all-done.1.in_ref = f32[8,192,128]{2,1,0:T(8,128)S(1)} async-done(((f32[8,192,128]{2,1,0:T(8,128)}), f32[8,192,128]{2,1,0:T(8,128)S(1)}, u32[]{:S(2)}, u32[]{:S(2)}) %all-to-all-start.1) | async-done | bytes 786464 | tf_op jit(solution)/shard_map/all_to_all | solution.py:119
  41.2 0.8 %partial.1 = f32[64,1,128]{2,1,0:T(1,128)} custom-call(f32[2,8,128,128]{3,2,1,0:T(8,128)S(1)} %mixed.1.mixed_ref, f32[8,192,128]{2,1,0:T(8,128)S(1)} %all-to-all-done.1.in_ref), custom_call_target="tpu_custom_call" | custom-call | tf_op jit(solution)/shard_map/partial/pallas_call | solution.py:153
  42.0 5.6 %all-to-all-start.2 = ((f32[64,1,128]{2,1,0:T(1,128)}), f32[64,1,128]{2,1,0:T(1,128)S(1)}, u32[]{:S(2)}, u32[]{:S(2)}) async-start(f32[64,1,128]{2,1,0:T(1,128)} %partial.1), calls=%async_computation.2 | async-start | bytes 65536 | tf_op jit(solution)/shard_map/all_to_all | solution.py:119
  47.7 5.4 %factor.1.inverse_ref = f32[64,64]{1,0:T(8,128)S(1)} custom-call(f32[8,192,128]{2,1,0:T(8,128)S(1)} %all-to-all-done.1.in_ref), custom_call_target="tpu_custom_call" | custom-call | flops 4000000000 | bytes 800000 | tf_op jit(solution)/shard_map/factor/pallas_call | solution.py:155
  53.1 6.5 %all-to-all-done.2.in_ref = f32[64,1,128]{2,1,0:T(1,128)S(1)} async-done(((f32[64,1,128]{2,1,0:T(1,128)}), f32[64,1,128]{2,1,0:T(1,128)S(1)}, u32[]{:S(2)}, u32[]{:S(2)}) %all-to-all-start.2) | async-done | bytes 32800 | tf_op jit(solution)/shard_map/all_to_all | solution.py:119
  59.6 1.0 %last.1 = f32[2,64]{1,0:T(2,128)} custom-call(f32[64,1,128]{2,1,0:T(1,128)S(1)} %all-to-all-done.2.in_ref, f32[64,64]{1,0:T(8,128)S(1)} %factor.1.inverse_ref), custom_call_target="tpu_custom_call" | custom-call | tf_op jit(solution)/shard_map/last/pallas_call | solution.py:162
Async XLA Ops:
  0.0 0.8 %copy-start.1 = (f32[256,64]{0,1:T(8,128)S(1)}, f32[256,64]{0,1:T(8,128)}, u32[]{:S(2)}) copy-start(f32[256,64]{0,1:T(8,128)} %param.4) | copy-start | bytes 196612
  0.8 0.8 %copy-start.2 = (f32[64,64]{1,0:T(8,128)S(1)}, f32[64,64]{1,0:T(8,128)}, u32[]{:S(2)}) copy-start(f32[64,64]{1,0:T(8,128)} %c_ref.1) | copy-start | bytes 49156
  23.3 18.0 %all-to-all-start.1 = ((f32[8,192,128]{2,1,0:T(8,128)}), f32[8,192,128]{2,1,0:T(8,128)S(1)}, u32[]{:S(2)}, u32[]{:S(2)}) async-start(f32[8,192,128]{2,1,0:T(8,128)} %get-tuple-element.8), calls=%async_computation.1 | async-start | bytes 1572864 | tf_op jit(solution)/shard_map/all_to_all | solution.py:119
  29.3 3.4 %copy-start = (f32[2,2048,512]{2,1,0:T(8,128)S(1)}, f32[2,2048,512]{2,1,0:T(8,128)}, u32[]{:S(2)}) copy-start(f32[2,2048,512]{2,1,0:T(8,128)} %t_ref.1) | copy-start | bytes 25165828
  42.0 17.6 %all-to-all-start.2 = ((f32[64,1,128]{2,1,0:T(1,128)}), f32[64,1,128]{2,1,0:T(1,128)S(1)}, u32[]{:S(2)}, u32[]{:S(2)}) async-start(f32[64,1,128]{2,1,0:T(1,128)} %partial.1), calls=%async_computation.2 | async-start | bytes 65536 | tf_op jit(solution)/shard_map/all_to_all | solution.py:119

commit v3 on v0

v3 whole, which is shorter than its diff:
```python
import jax
import jax.numpy as jnp
from jax import lax
from jax.experimental import pallas as pl
from jax.experimental.pallas import tpu as pltpu
from jax.sharding import PartitionSpec as P

F32, BF16 = jnp.float32, jnp.bfloat16
HIGHEST = lax.Precision.HIGHEST
VMEM = pl.BlockSpec(memory_space=pltpu.VMEM)
ANY = pl.BlockSpec(memory_space=pl.ANY)
LIMIT = 24 * 1024 * 1024
ROWS, SLOTS = 1024, 3


def pieces(x, n):
    out = []
    for _ in range(n - 1):
        out.append(x.astype(BF16))
        x = x - out[-1].astype(F32)
    return out + [x.astype(BF16)]


def product(x, y, dim):
    xs, ys = pieces(x, 3), pieces(y, 3)
    return sum(
        lax.dot_general(a, b, (((dim,), (dim,)), ((), ())), preferred_element_type=F32)
        for n, a in enumerate(xs)
        for b in ys[: 3 - n]
    )


def fold(x, axis=0):
    half = x.shape[axis] // 2
    index = [slice(None)] * x.ndim
    upper, lower = list(index), list(index)
    upper[axis], lower[axis] = slice(0, half), slice(half, None)
    return jnp.concatenate([x[tuple(upper)], x[tuple(lower)]], axis=-1)


def unfold(x):
    rank = x.shape[-1] // 2
    return jnp.concatenate([x[..., :rank], x[..., rank:]], axis=-2)


def quarter():
    return jnp.bitwise_xor(lax.axis_index("rows"), lax.axis_index("pods") % 2 * (lax.axis_size("rows") // 2))


def first_kernel(bt_ref, c_ref, out_ref, b_ref, bt, c, sems):
    copies = [
        pltpu.make_async_copy(source, to, sems.at[n]) for n, (source, to) in enumerate(((bt_ref, bt), (c_ref, c)))
    ]
    for copy in copies:
        copy.start()
    copies[0].wait()
    half = b_ref.shape[0]
    b_ref[...] = jnp.concatenate([bt[:, :half].T, bt[:, half:].T], axis=1)
    share = bt.shape[0] // lax.axis_size("rows")
    at = pl.ds(pl.multiple_of(quarter() * share, share), share)
    gram_b = fold(product(bt[at], bt[...], 1))
    copies[1].wait()
    block = jnp.concatenate([fold(c[...]), gram_b], axis=0)
    for n in range(out_ref.shape[0]):
        out_ref[n] = block


def second_kernel(b_ref, in_ref, out_ref, gram, grams, sems):
    rank = gram.shape[0]
    half, own = b_ref.shape[0], grams.shape[0] // 2
    rows = in_ref.shape[1] - own
    copies = []
    for n in range(out_ref.shape[0]):
        copies.append(pltpu.make_async_copy(b_ref, out_ref.at[n, pl.ds(0, half)], sems.at[0, n]))
        copies[-1].start()
    c = in_ref[:, :rows].reshape(-1, 2 * rank)
    both = product(c, c, 0)
    gram[...] = both[:rank, :rank] + both[rank:, rank:]
    at = pl.ds(pl.multiple_of(quarter() * 2 * own, 2 * own), 2 * own)
    grams[:own] = fold(gram[at])
    grams[own:] = jnp.sum(in_ref[:, rows:], axis=0)
    for n in range(out_ref.shape[0]):
        copies.append(pltpu.make_async_copy(grams, out_ref.at[n, pl.ds(half, 2 * own)], sems.at[1, n]))
        copies[-1].start()
    for copy in copies:
        copy.wait()


def mixed_kernel(t_ref, c_ref, out_ref, buffer, sems):
    slots, step, extent = buffer.shape
    devices, _, width = c_ref.shape
    rank = width // 2
    each = t_ref.shape[1] // step
    steps = t_ref.shape[0] * each

    def copy(n):
        at = pl.ds(pl.multiple_of(n % each * step, step), step)
        return pltpu.make_async_copy(t_ref.at[n // each, at], buffer.at[n % slots], sems.at[n % slots])

    for n in range(slots):
        copy(n).start()
    c = unfold(c_ref[:, : extent // devices // 2]).reshape(extent, rank)
    w = jnp.concatenate(pieces(c, 2), axis=1)
    half = out_ref.shape[2]
    left = lax.broadcasted_iota(jnp.int32, (half, width), 1) < rank

    def work(n, carry):
        copy(n).wait()
        high, low = pieces(buffer[n % slots], 2)
        both = jnp.dot(high, w, preferred_element_type=F32) + jnp.dot(low, w, preferred_element_type=F32)

        @pl.when(n + slots < steps)
        def _():
            copy(n + slots).start()

        both = both + pltpu.roll(both, rank, 1)
        for m in range(step // (2 * half)):
            part = both[2 * half * m : 2 * half * (m + 1)]
            out_ref[n // each, n % each * (step // (2 * half)) + m] = jnp.where(left, part[:half], part[half:])
        return carry

    lax.fori_loop(0, steps, work, 0)


def partial_kernel(mixed_ref, in_ref, out_ref):
    half = mixed_ref.shape[2]
    width = mixed_ref.shape[3]
    rows = []
    for i in range(2):
        total = jnp.zeros((8, width), F32)
        for n in range(mixed_ref.shape[1]):
            each = mixed_ref[i, n] * in_ref[n, :half]
            total = total + jnp.sum(each.reshape(half // 8, 8, width), axis=0)
        row = jnp.sum(total, axis=0, keepdims=True)
        rows.append(row + pltpu.roll(row, width // 2, 1))
    left = lax.broadcasted_iota(jnp.int32, (1, width), 1) < width // 2
    out_ref[...] = jnp.broadcast_to(jnp.where(left, rows[0], rows[1]), out_ref.shape)


def normal_kernel(in_ref, partial_ref, out_ref):
    own = out_ref.shape[0]
    grams = jnp.sum(in_ref[:, in_ref.shape[1] - 2 * own :], axis=0)
    out_ref[...] = grams[:own] * grams[own:]


def factor_kernel(*refs):
    parts, out_ref, (normal, inverse) = refs[:-3], refs[-3], refs[-2:]
    rank = normal.shape[0]
    share = rank // len(parts)
    me = quarter()
    for n, part in enumerate(parts):
        at = pl.ds(pl.multiple_of(jnp.bitwise_xor(me, n) * share, share), share)
        normal[at] = unfold(part[...])
    a = normal[...]
    eye = lax.broadcasted_iota(jnp.int32, (rank, rank), 0) == lax.broadcasted_iota(jnp.int32, (rank, rank), 1)
    a = jnp.concatenate([a, eye.astype(F32)], axis=1)
    row_at = lax.broadcasted_iota(jnp.int32, a.shape, 0)
    for k in range(rank):
        row = a[k : k + 1]
        column = a[:, k : k + 1]
        scale = lax.rsqrt(row[:, k : k + 1])
        row = row * scale
        inverse[k : k + 1] = row[:, rank:]
        a = jnp.where(row_at > k, a - (column * scale) * row, a)
    root = inverse[...]
    full = lax.dot_general(root, root, (((0,), (0,)), ((), ())), precision=HIGHEST, preferred_element_type=F32)
    out_ref[...] = jnp.concatenate(pieces(full, 3), axis=1)


def last_kernel(in_ref, inverse_ref, out_ref):
    rank = inverse_ref.shape[0]
    total = jnp.sum(in_ref[...], axis=0, keepdims=True)
    x = jnp.concatenate([total[:, :rank], total[:, rank:]], axis=0)
    parts = jnp.dot(jnp.concatenate(pieces(x, 3), axis=0), inverse_ref[...], preferred_element_type=F32)
    out_ref[...] = sum(
        parts[2 * n : 2 * n + 2, m * rank : (m + 1) * rank] for n in reversed(range(3)) for m in reversed(range(3 - n))
    )


def call(kernel, name, ins, outs, scratch=(), out=VMEM, **more):
    return pl.pallas_call(
        kernel,
        name=name,
        in_specs=ins,
        out_specs=out,
        out_shape=outs,
        scratch_shapes=scratch,
        compiler_params=pltpu.CompilerParams(vmem_limit_bytes=LIMIT),
        **more,
    )


def exchange(x, axes, groups=None):
    return lax.all_to_all(x, axes, 0, 0, tiled=True, axis_index_groups=groups)


def body(groups, tensor, factor_b, factor_c):
    rows, racks, pods = (lax.axis_size(axis) for axis in ("rows", "racks", "pods"))
    slabs, extent_j, extent_k = tensor.shape
    own_b, rank = factor_b.shape
    own_c = factor_c.shape[0]
    half, width, own = own_b // 2, 2 * rank, rank // rows // 2
    shape, fast = jax.ShapeDtypeStruct, pltpu.VMEM
    tensor, bt, factor_c = (pltpu.with_memory_space_constraint(x, pltpu.HBM) for x in (tensor, factor_b.T, factor_c))

    first, b = call(
        first_kernel,
        "first",
        [ANY, ANY],
        [fast((racks, own_c // 2 + own, width), F32), fast((half, width), F32)],
        [pltpu.VMEM(bt.shape, F32), pltpu.VMEM(factor_c.shape, F32), pltpu.SemaphoreType.DMA((2,))],
        [VMEM, VMEM],
    )(bt, factor_c)
    first = exchange(first, "racks")
    second = call(
        second_kernel,
        "second",
        [VMEM, VMEM],
        shape((pods, half + 2 * own, width), F32),
        [pltpu.VMEM((rank, rank), F32), pltpu.VMEM((2 * own, width), F32), pltpu.SemaphoreType.DMA((2, pods))],
        ANY,
    )(b, first)
    second = exchange(second, ("rows", "racks", "pods"), groups)
    mixed = call(
        mixed_kernel,
        "mixed",
        [ANY, VMEM],
        fast((slabs, pods, half, width), F32),
        [pltpu.VMEM((SLOTS, ROWS, extent_k), F32), pltpu.SemaphoreType.DMA((SLOTS,))],
        cost_estimate=pl.CostEstimate(
            flops=4 * tensor.size * width, bytes_accessed=4 * tensor.size, transcendentals=0
        ),
    )(tensor, first)
    partial = call(partial_kernel, "partial", [VMEM, VMEM], shape((racks * pods, width), F32))(mixed, second)
    everyone = exchange(partial.reshape(racks * pods, 1, width), ("racks", "pods"))
    normal = call(
        normal_kernel,
        "normal",
        [VMEM, ANY],
        shape((own, width), F32),
        cost_estimate=pl.CostEstimate(flops=1_000_000, bytes_accessed=80_000, transcendentals=0),
    )(second, partial)
    normals = [normal] + [lax.ppermute(normal, "rows", [(r, r ^ n) for r in range(rows)]) for n in range(1, rows)]
    inverse = call(
        factor_kernel,
        "factor",
        [VMEM] * rows,
        shape((rank, 3 * rank), BF16),
        [pltpu.VMEM((rank, rank), F32), pltpu.VMEM((rank, rank), F32)],
        cost_estimate=pl.CostEstimate(flops=1_000_000, bytes_accessed=80_000, transcendentals=64),
    )(*normals)
    return call(last_kernel, "last", [VMEM, VMEM], shape((slabs, rank), F32))(
        everyone.reshape(racks * pods, width), inverse
    )


def nearest_pods(mesh):
    rows, racks, pods = (mesh.shape[axis] for axis in ("rows", "racks", "pods"))
    return [
        [((low ^ (p % 2)) * (rows // 2) + core) * racks * pods + z * pods + p for p in range(pods)]
        for low in range(2)
        for core in range(rows // 2)
        for z in range(racks)
    ]


def solution(mesh):
    groups = nearest_pods(mesh)

    def mapped(tensor, factor_b, factor_c):
        return body(groups, tensor, factor_b, factor_c)

    in_specs = (P("rows", "racks", "pods"), P(("racks", "pods"), None), P(("pods", "racks"), None))
    out_specs = P("rows", None)
    return jax.shard_map(mapped, mesh=mesh, in_specs=in_specs, out_specs=out_specs, check_vma=False)
```

time: 446 us -> 55.3 us (0.12)
  blocking collectives: 421 us -> 18 us
  Pallas kernels: 0 us -> 14.6 us
  starting transfers between devices: 0 us -> 14.4 us
  matrix products: 12.2 us -> 0 us
  other arithmetic: 12.1 us -> 0 us
  waiting for transfers between devices: 0 us -> 7.97 us
    psum x1 -> x0, blocking collectives: 357 us -> none  [body(): lax.psum((gram_b_part, gram_c_part, partial_sum), ('racks', 'pods'))]
    all_gather x2 -> x0, blocking collectives: 64 us -> none  [the longest x1 35.4 us: body(): lax.all_gather(factor_b, 'pods', axis=0, tiled=True)[None]]
    all_to_all x0 -> x1, blocking collectives: none -> 18 us  [exchange(): return lax.all_to_all(x, axes, 0, 0, tiled=True, axis_index_groups=groups)]
    pallas_call x0 -> x7, Pallas kernels: none -> 14.6 us  [the longest x1 5.74 us: body(): call(factor_kernel, 'factor', [VMEM] * rows, shape((rank, 3 * rank), BF16...]
    all_to_all x0 -> x2, starting transfers between devices: none -> 12.5 us  [exchange(): return lax.all_to_all(x, axes, 0, 0, tiled=True, axis_index_groups=groups)]
    another operation x5 -> x0, other arithmetic: 12.1 us -> none  [the longest x3 6.52 us: body(): lower = jnp.linalg.cholesky(gram_b * gram_c)]
    dot_general x3 -> x0, matrix products: 11.1 us -> none  [the longest x1 10.7 us: body(): jnp.einsum('ijk,kr->ijr', tensor, c_block, precision=highest, preferred_e...]
    all_to_all x0 -> x2, waiting for transfers between devices: none -> 6.12 us  [exchange(): return lax.all_to_all(x, axes, 0, 0, tiled=True, axis_index_groups=groups)]
  transfers between devices with their start and end apart: 0 -> 5, of which waited for: 0 -> 4; matrix products, arithmetic and copies ran while one was open for 0% -> 0% of each run, Pallas kernels for 0% -> 19%
where the time goes in v3:
time: 55.3 us; the launch traced here: 55.1 us
  blocking collectives  18 us (33%)
  Pallas kernels  14.6 us (26%)
  starting transfers between devices  14.4 us (26%)
  waiting for transfers between devices  7.97 us (14%)
    all_to_all x1, blocking collectives, exchange(): return lax.all_to_all(x, axes, 0, 0, tiled=True, axis_index_groups=groups)  18 us
    all_to_all x2, starting transfers between devices, exchange(): return lax.all_to_all(x, axes, 0, 0, tiled=True, axis_index_groups=groups)  12.5 us
    all_to_all x2, waiting for transfers between devices, exchange(): return lax.all_to_all(x, axes, 0, 0, tiled=True, axis_index_groups=groups)  6.12 us
    pallas_call x1, Pallas kernels, body(): call(factor_kernel, 'factor', [VMEM] * rows, shape((rank, 3 * rank), BF16...  5.74 us
    pallas_call x1, Pallas kernels, body(): call(mixed_kernel, 'mixed', [ANY, VMEM], fast((slabs, pods, half, width),...  4.81 us
    ppermute x3, starting transfers between devices, body(): lax.ppermute(normal, 'rows', [(r, r ^ n) for r in range(rows)])  1.94 us
    ppermute x3, waiting for transfers between devices, body(): lax.ppermute(normal, 'rows', [(r, r ^ n) for r in range(rows)])  1.85 us
    pallas_call x1, Pallas kernels, body(): call(second_kernel, 'second', [VMEM, VMEM], shape((pods, half + 2 * own,...  1.23 us
  transfers between devices with their start and end apart: 5, of which 4 were waited for; matrix products, arithmetic and copies ran while one was open for 0% of the time, Pallas kernels for 19%

profile of v3, /device:TPU:8, one launch (start us, length us, event | category | flops | bytes accessed | tf_op | source)
XLA Modules:
  0.0 55.1 jit_solution(13386002699356041810)
XLA Ops:
  0.0 1.2 %first.1 = (f32[8,40,128]{2,1,0:T(8,128)S(1)}, f32[128,128]{1,0:T(8,128)S(1)}) custom-call(f32[64,256]{1,0:T(8,128)} %bitcast.6, f32[64,64]{1,0:T(8,128)} %c_ref.1), custom_call_target="tpu_custom_call" | custom-call | tf_op jit(solution)/shard_map/first/pallas_call | solution.py:206
  1.2 18.0 %all_to_all.15.c_ref.in_ref = f32[8,40,128]{2,1,0:T(8,128)S(1)} all-to-all(f32[8,40,128]{2,1,0:T(8,128)S(1)} %get-tuple-element.7), channel_id=1, replica_groups=mesh['rows'=4,'racks'=8,'pods'=8] {'racks'}, dimensions={0} | all-to-all | bytes 327680 | tf_op jit(solution)/shard_map/all_to_all | solution.py:194
  19.2 1.2 %second.1 = f32[8,144,128]{2,1,0:T(8,128)} custom-call(f32[128,128]{1,0:T(8,128)S(1)} %get-tuple-element.8.b_ref, f32[8,40,128]{2,1,0:T(8,128)S(1)} %all_to_all.15.c_ref.in_ref), custom_call_target="tpu_custom_call" | custom-call | tf_op jit(solution)/shard_map/second/pallas_call | solution.py:215
  20.5 5.3 %all-to-all-start.1 = ((f32[8,144,128]{2,1,0:T(8,128)}), f32[8,144,128]{2,1,0:T(8,128)S(1)}, u32[]{:S(2)}, u32[]{:S(2)}) async-start(f32[8,144,128]{2,1,0:T(8,128)} %second.1), calls=%async_computation.1 | async-start | bytes 1179648 | tf_op jit(solution)/shard_map/all_to_all | solution.py:194
  25.8 4.8 %mixed.1.mixed_ref = f32[2,8,128,128]{3,2,1,0:T(8,128)S(1)} custom-call(f32[2,2048,512]{2,1,0:T(8,128)} %t_ref.1, f32[8,40,128]{2,1,0:T(8,128)S(1)} %all_to_all.15.c_ref.in_ref), custom_call_target="tpu_custom_call" | custom-call | flops 1073741824 | bytes 8388608 | tf_op jit(solution)/shard_map/mixed/pallas_call | solution.py:224
  30.6 3.7 %all-to-all-done.1.in_ref = f32[8,144,128]{2,1,0:T(8,128)S(1)} async-done(((f32[8,144,128]{2,1,0:T(8,128)}), f32[8,144,128]{2,1,0:T(8,128)S(1)}, u32[]{:S(2)}, u32[]{:S(2)}) %all-to-all-start.1) | async-done | bytes 589856 | tf_op jit(solution)/shard_map/all_to_all | solution.py:194
  34.3 0.8 %partial.1.partial_ref = f32[64,128]{1,0:T(8,128)} custom-call(f32[2,8,128,128]{3,2,1,0:T(8,128)S(1)} %mixed.1.mixed_ref, f32[8,144,128]{2,1,0:T(8,128)S(1)} %all-to-all-done.1.in_ref), custom_call_target="tpu_custom_call" | custom-call | tf_op jit(solution)/shard_map/partial/pallas_call | solution.py:234
  35.1 7.2 %all-to-all-start.2 = ((f32[64,1,128]{2,1,0:T(1,128)}), f32[64,1,128]{2,1,0:T(1,128)S(1)}, u32[]{:S(2)}, u32[]{:S(2)}) async-start(f32[64,1,128]{2,1,0:T(1,128)} %bitcast.2), calls=%async_computation.2 | async-start | bytes 65536 | tf_op jit(solution)/shard_map/all_to_all | solution.py:194
  42.3 0.1 collective-permute-start.2
  42.4 0.7 %collective-permute-start.1 = (f32[8,128]{1,0:T(8,128)S(1)}, f32[8,128]{1,0:T(8,128)S(1)}, u32[]{:S(2)}, u32[]{:S(2)}) collective-permute-start(f32[8,128]{1,0:T(8,128)S(1)} %normal.1.refs_0_), channel_id=1, source_target_pairs={{0,128},{64,192},{128,0},{192,64},{1,129},{65,193},{129,1},{193,65... | collective-permute-start | bytes 12296 | tf_op jit(solution)/shard_map/ppermute | solution.py:243
  43.1 1.1 %collective-permute-start = (f32[8,128]{1,0:T(8,128)S(1)}, f32[8,128]{1,0:T(8,128)S(1)}, u32[]{:S(2)}, u32[]{:S(2)}) collective-permute-start(f32[8,128]{1,0:T(8,128)S(1)} %normal.1.refs_0_), channel_id=1, source_target_pairs={{0,64},{64,0},{128,192},{192,128},{1,65},{65,1},{129,193},{193,129... | collective-permute-start | bytes 12296 | tf_op jit(solution)/shard_map/ppermute | solution.py:243
  44.2 1.2 %collective-permute-done.2.refs_3_ = f32[8,128]{1,0:T(8,128)S(1)} collective-permute-done((f32[8,128]{1,0:T(8,128)S(1)}, f32[8,128]{1,0:T(8,128)S(1)}, u32[]{:S(2)}, u32[]{:S(2)}) %collective-permute-start.2) | collective-permute-done | bytes 4128 | tf_op jit(solution)/shard_map/ppermute | solution.py:243
  45.4 0.7 %collective-permute-done.1.refs_2_ = f32[8,128]{1,0:T(8,128)S(1)} collective-permute-done((f32[8,128]{1,0:T(8,128)S(1)}, f32[8,128]{1,0:T(8,128)S(1)}, u32[]{:S(2)}, u32[]{:S(2)}) %collective-permute-start.1) | collective-permute-done | bytes 4128 | tf_op jit(solution)/shard_map/ppermute | solution.py:243
  46.1 0.0 collective-permute-done.refs_1_
  46.1 5.7 %factor.1.inverse_ref = bf16[64,192]{1,0:T(8,128)(2,1)S(1)} custom-call(f32[8,128]{1,0:T(8,128)S(1)} %normal.1.refs_0_, f32[8,128]{1,0:T(8,128)S(1)} %collective-permute-done.refs_1_, f32[8,128]{1,0:T(8,128)S(1)} %collective-permute-done.1.refs_2_, f32[8,128]{1,0:T(8,128)S(1)} %collective-permute-done.2.refs_3_), custom_call_target="tpu_custom_call" | custom-call | flops 1000000 | bytes 80000 | tf_op jit(solution)/shard_map/factor/pallas_call | solution.py:244
  51.8 2.4 %all-to-all-done.2 = f32[64,1,128]{2,1,0:T(1,128)S(1)} async-done(((f32[64,1,128]{2,1,0:T(1,128)}), f32[64,1,128]{2,1,0:T(1,128)S(1)}, u32[]{:S(2)}, u32[]{:S(2)}) %all-to-all-start.2) | async-done | bytes 32800 | tf_op jit(solution)/shard_map/all_to_all | solution.py:194
  54.2 0.8 %last.1 = f32[2,64]{1,0:T(2,128)} custom-call(f32[64,128]{1,0:T(8,128)S(1)} %bitcast.5, bf16[64,192]{1,0:T(8,128)(2,1)S(1)} %factor.1.inverse_ref), custom_call_target="tpu_custom_call" | custom-call | tf_op jit(solution)/shard_map/last/pallas_call | solution.py:252
  (1 shorter events, 0.0 us)
Async XLA Ops:
  20.5 13.9 %all-to-all-start.1 = ((f32[8,144,128]{2,1,0:T(8,128)}), f32[8,144,128]{2,1,0:T(8,128)S(1)}, u32[]{:S(2)}, u32[]{:S(2)}) async-start(f32[8,144,128]{2,1,0:T(8,128)} %second.1), calls=%async_computation.1 | async-start | bytes 1179648 | tf_op jit(solution)/shard_map/all_to_all | solution.py:194
  35.1 19.1 %all-to-all-start.2 = ((f32[64,1,128]{2,1,0:T(1,128)}), f32[64,1,128]{2,1,0:T(1,128)S(1)}, u32[]{:S(2)}, u32[]{:S(2)}) async-start(f32[64,1,128]{2,1,0:T(1,128)} %bitcast.2), calls=%async_computation.2 | async-start | bytes 65536 | tf_op jit(solution)/shard_map/all_to_all | solution.py:194
  42.3 3.1 %collective-permute-start.2 = (f32[8,128]{1,0:T(8,128)S(1)}, f32[8,128]{1,0:T(8,128)S(1)}, u32[]{:S(2)}, u32[]{:S(2)}) collective-permute-start(f32[8,128]{1,0:T(8,128)S(1)} %normal.1.refs_0_), channel_id=1, source_target_pairs={{0,192},{64,128},{128,64},{192,0},{1,193},{65,129},{129,65},{193,1... | collective-permute-start | bytes 12296 | tf_op jit(solution)/shard_map/ppermute | solution.py:243
  42.4 3.7 %collective-permute-start.1 = (f32[8,128]{1,0:T(8,128)S(1)}, f32[8,128]{1,0:T(8,128)S(1)}, u32[]{:S(2)}, u32[]{:S(2)}) collective-permute-start(f32[8,128]{1,0:T(8,128)S(1)} %normal.1.refs_0_), channel_id=1, source_target_pairs={{0,128},{64,192},{128,0},{192,64},{1,129},{65,193},{129,1},{193,65... | collective-permute-start | bytes 12296 | tf_op jit(solution)/shard_map/ppermute | solution.py:243
  43.1 3.0 %collective-permute-start = (f32[8,128]{1,0:T(8,128)S(1)}, f32[8,128]{1,0:T(8,128)S(1)}, u32[]{:S(2)}, u32[]{:S(2)}) collective-permute-start(f32[8,128]{1,0:T(8,128)S(1)} %normal.1.refs_0_), channel_id=1, source_target_pairs={{0,64},{64,0},{128,192},{192,128},{1,65},{65,1},{129,193},{193,129... | collective-permute-start | bytes 12296 | tf_op jit(solution)/shard_map/ppermute | solution.py:243

commit v4 on v3

--- a/solution.py
+++ b/solution.py
@@ -1,3 +1,5 @@
+import functools
+
 import jax
 import jax.numpy as jnp
 from jax import lax
@@ -11,6 +13,7 @@
 ANY = pl.BlockSpec(memory_space=pl.ANY)
 LIMIT = 24 * 1024 * 1024
 ROWS, SLOTS = 1024, 3
+EARLY = 96
 
 
 def pieces(x, n):
@@ -43,8 +46,12 @@
     return jnp.concatenate([x[..., :rank], x[..., rank:]], axis=-2)
 
 
-def quarter():
-    return jnp.bitwise_xor(lax.axis_index("rows"), lax.axis_index("pods") % 2 * (lax.axis_size("rows") // 2))
+def half_label():
+    return jnp.bitwise_xor(lax.axis_index("rows") // 2, lax.axis_index("pods") % 2)
+
+
+def gathers_b():
+    return lax.axis_index("rows") % 2 == 0
 
 
 def first_kernel(bt_ref, c_ref, out_ref, b_ref, bt, c, sems):
@@ -56,39 +63,45 @@
     copies[0].wait()
     half = b_ref.shape[0]
     b_ref[...] = jnp.concatenate([bt[:, :half].T, bt[:, half:].T], axis=1)
-    share = bt.shape[0] // lax.axis_size("rows")
-    at = pl.ds(pl.multiple_of(quarter() * share, share), share)
+    share = bt.shape[0] // 2
+    at = pl.ds(pl.multiple_of(half_label() * share, share), share)
     gram_b = fold(product(bt[at], bt[...], 1))
     copies[1].wait()
-    block = jnp.concatenate([fold(c[...]), gram_b], axis=0)
+    other = jnp.concatenate([fold(c[...]), gram_b], axis=0)
+    rows = out_ref.shape[1]
+    other = jnp.concatenate([other, jnp.zeros((rows - other.shape[0], other.shape[1]), F32)], axis=0)
+    block = jnp.where(gathers_b(), b_ref[:rows], other)
     for n in range(out_ref.shape[0]):
         out_ref[n] = block
 
 
-def second_kernel(b_ref, in_ref, out_ref, gram, grams, sems):
+def second_kernel(rows, b_ref, in_ref, out_ref, gram, grams, sems):
     rank = gram.shape[0]
-    half, own = b_ref.shape[0], grams.shape[0] // 2
-    rows = in_ref.shape[1] - own
+    own = grams.shape[0] // 2
+    first = in_ref.shape[1]
+    rest = b_ref.shape[0] - first
     copies = []
     for n in range(out_ref.shape[0]):
-        copies.append(pltpu.make_async_copy(b_ref, out_ref.at[n, pl.ds(0, half)], sems.at[0, n]))
+        copies.append(
+            pltpu.make_async_copy(b_ref.at[pl.ds(first, rest)], out_ref.at[n, pl.ds(0, rest)], sems.at[0, n])
+        )
         copies[-1].start()
     c = in_ref[:, :rows].reshape(-1, 2 * rank)
     both = product(c, c, 0)
     gram[...] = both[:rank, :rank] + both[rank:, rank:]
-    at = pl.ds(pl.multiple_of(quarter() * 2 * own, 2 * own), 2 * own)
+    at = pl.ds(pl.multiple_of(half_label() * 2 * own, 2 * own), 2 * own)
     grams[:own] = fold(gram[at])
-    grams[own:] = jnp.sum(in_ref[:, rows:], axis=0)
+    grams[own:] = jnp.sum(in_ref[:, rows : rows + own], axis=0)
     for n in range(out_ref.shape[0]):
-        copies.append(pltpu.make_async_copy(grams, out_ref.at[n, pl.ds(half, 2 * own)], sems.at[1, n]))
+        copies.append(pltpu.make_async_copy(grams, out_ref.at[n, pl.ds(rest, 2 * own)], sems.at[1, n]))
         copies[-1].start()
     for copy in copies:
         copy.wait()
 
 
-def mixed_kernel(t_ref, c_ref, out_ref, buffer, sems):
+def mixed_kernel(t_ref, own_ref, other_ref, out_ref, buffer, sems):
     slots, step, extent = buffer.shape
-    devices, _, width = c_ref.shape
+    devices, _, width = own_ref.shape
     rank = width // 2
     each = t_ref.shape[1] // step
     steps = t_ref.shape[0] * each
@@ -99,7 +112,9 @@
 
     for n in range(slots):
         copy(n).start()
-    c = unfold(c_ref[:, : extent // devices // 2]).reshape(extent, rank)
+    rows = extent // devices // 2
+    c = jnp.where(gathers_b(), other_ref[:, :rows], own_ref[:, :rows])
+    c = unfold(c).reshape(extent, rank)
     w = jnp.concatenate(pieces(c, 2), axis=1)
     half = out_ref.shape[2]
     left = lax.broadcasted_iota(jnp.int32, (half, width), 1) < rank
@@ -122,15 +137,19 @@
     lax.fori_loop(0, steps, work, 0)
 
 
-def partial_kernel(mixed_ref, in_ref, out_ref):
+def partial_kernel(mixed_ref, own_ref, other_ref, in_ref, out_ref):
     half = mixed_ref.shape[2]
     width = mixed_ref.shape[3]
+    first = own_ref.shape[1]
+    mine = gathers_b()
+    totals = [jnp.zeros((8, width), F32) for _ in range(2)]
+    for n in range(mixed_ref.shape[1]):
+        b = jnp.where(mine, own_ref[n], other_ref[n])
+        b = jnp.concatenate([b, in_ref[n, : half - first]], axis=0)
+        for i in range(2):
+            totals[i] = totals[i] + jnp.sum((mixed_ref[i, n] * b).reshape(half // 8, 8, width), axis=0)
     rows = []
-    for i in range(2):
-        total = jnp.zeros((8, width), F32)
-        for n in range(mixed_ref.shape[1]):
-            each = mixed_ref[i, n] * in_ref[n, :half]
-            total = total + jnp.sum(each.reshape(half // 8, 8, width), axis=0)
+    for total in totals:
         row = jnp.sum(total, axis=0, keepdims=True)
         rows.append(row + pltpu.roll(row, width // 2, 1))
     left = lax.broadcasted_iota(jnp.int32, (1, width), 1) < width // 2
@@ -146,11 +165,12 @@
 def factor_kernel(*refs):
     parts, out_ref, (normal, inverse) = refs[:-3], refs[-3], refs[-2:]
     rank = normal.shape[0]
-    share = rank // len(parts)
-    me = quarter()
-    for n, part in enumerate(parts):
+    share = rank // 2
+    me = half_label()
+    own, core, chip, both = (part[...] for part in parts)
+    for n, part in enumerate((jnp.where(gathers_b(), core, own), jnp.where(gathers_b(), both, chip))):
         at = pl.ds(pl.multiple_of(jnp.bitwise_xor(me, n) * share, share), share)
-        normal[at] = unfold(part[...])
+        normal[at] = unfold(part)
     a = normal[...]
     eye = lax.broadcasted_iota(jnp.int32, (rank, rank), 0) == lax.broadcasted_iota(jnp.int32, (rank, rank), 1)
     a = jnp.concatenate([a, eye.astype(F32)], axis=1)
@@ -194,12 +214,13 @@
     return lax.all_to_all(x, axes, 0, 0, tiled=True, axis_index_groups=groups)
 
 
-def body(groups, tensor, factor_b, factor_c):
-    rows, racks, pods = (lax.axis_size(axis) for axis in ("rows", "racks", "pods"))
+def body(gather_groups, pods_groups, tensor, factor_b, factor_c):
+    axes = ("rows", "racks", "pods")
+    rows, racks, pods = (lax.axis_size(axis) for axis in axes)
     slabs, extent_j, extent_k = tensor.shape
     own_b, rank = factor_b.shape
     own_c = factor_c.shape[0]
-    half, width, own = own_b // 2, 2 * rank, rank // rows // 2
+    half, width, own = own_b // 2, 2 * rank, rank // 4
     shape, fast = jax.ShapeDtypeStruct, pltpu.VMEM
     tensor, bt, factor_c = (pltpu.with_memory_space_constraint(x, pltpu.HBM) for x in (tensor, factor_b.T, factor_c))
 
@@ -207,31 +228,34 @@
         first_kernel,
         "first",
         [ANY, ANY],
-        [fast((racks, own_c // 2 + own, width), F32), fast((half, width), F32)],
+        [fast((racks, EARLY, width), F32), fast((half, width), F32)],
         [pltpu.VMEM(bt.shape, F32), pltpu.VMEM(factor_c.shape, F32), pltpu.SemaphoreType.DMA((2,))],
         [VMEM, VMEM],
     )(bt, factor_c)
-    first = exchange(first, "racks")
+    first = exchange(first, axes, gather_groups)
+    other = lax.ppermute(first, "rows", [(r, r ^ 1) for r in range(rows)])
     second = call(
-        second_kernel,
+        functools.partial(second_kernel, own_c // 2),
         "second",
         [VMEM, VMEM],
-        shape((pods, half + 2 * own, width), F32),
+        shape((pods, half - EARLY + 2 * own, width), F32),
         [pltpu.VMEM((rank, rank), F32), pltpu.VMEM((2 * own, width), F32), pltpu.SemaphoreType.DMA((2, pods))],
         ANY,
     )(b, first)
-    second = exchange(second, ("rows", "racks", "pods"), groups)
+    second = exchange(second, axes, pods_groups)
     mixed = call(
         mixed_kernel,
         "mixed",
-        [ANY, VMEM],
+        [ANY, VMEM, VMEM],
         fast((slabs, pods, half, width), F32),
         [pltpu.VMEM((SLOTS, ROWS, extent_k), F32), pltpu.SemaphoreType.DMA((SLOTS,))],
         cost_estimate=pl.CostEstimate(
             flops=4 * tensor.size * width, bytes_accessed=4 * tensor.size, transcendentals=0
         ),
-    )(tensor, first)
-    partial = call(partial_kernel, "partial", [VMEM, VMEM], shape((racks * pods, width), F32))(mixed, second)
+    )(tensor, first, other)
+    partial = call(partial_kernel, "partial", [VMEM] * 4, shape((racks * pods, width), F32))(
+        mixed, first, other, second
+    )
     everyone = exchange(partial.reshape(racks * pods, 1, width), ("racks", "pods"))
     normal = call(
         normal_kernel,
@@ -254,21 +278,25 @@
     )
 
 
-def nearest_pods(mesh):
+def groups_of(mesh):
     rows, racks, pods = (mesh.shape[axis] for axis in ("rows", "racks", "pods"))
-    return [
-        [((low ^ (p % 2)) * (rows // 2) + core) * racks * pods + z * pods + p for p in range(pods)]
-        for low in range(2)
-        for core in range(rows // 2)
-        for z in range(racks)
+
+    def device(low, core, z, p):
+        return ((low * 2 + core) * racks + z) * pods + p
+
+    lows = range(rows // 2)
+    by_pods = [
+        [[device(low ^ (p % 2), core, z, p) for p in range(pods)] for low in lows for z in range(racks)] for core in range(2)
     ]
+    by_racks = [[device(low, 1, z, p) for z in range(racks)] for low in lows for p in range(pods)]
+    return by_pods[0] + by_racks, by_pods[0] + by_pods[1]
 
 
 def solution(mesh):
-    groups = nearest_pods(mesh)
+    groups = groups_of(mesh)
 
     def mapped(tensor, factor_b, factor_c):
-        return body(groups, tensor, factor_b, factor_c)
+        return body(*groups, tensor, factor_b, factor_c)
 
     in_specs = (P("rows", "racks", "pods"), P(("racks", "pods"), None), P(("pods", "racks"), None))
     out_specs = P("rows", None)

time: 55.3 us -> 54.4 us (0.984)
  starting transfers between devices: 14.4 us -> 19.7 us
  blocking collectives: 18 us -> 12.9 us
  waiting for transfers between devices: 7.97 us -> 6.68 us
    ppermute x0 -> x1, starting transfers between devices: none -> 5.63 us  [body(): other = lax.ppermute(first, 'rows', [(r, r ^ 1) for r in range(rows)])]
    all_to_all x1, blocking collectives: 18 us -> 12.9 us  [exchange(): return lax.all_to_all(x, axes, 0, 0, tiled=True, axis_index_groups=groups)]
    all_to_all x2, waiting for transfers between devices: 6.12 us -> 4.79 us  [exchange(): return lax.all_to_all(x, axes, 0, 0, tiled=True, axis_index_groups=groups)]
  transfers between devices with their start and end apart: 5 -> 6, of which waited for: 4 -> 4; matrix products, arithmetic and copies ran while one was open for 0% -> 0% of each run, Pallas kernels for 19% -> 22%
where the time goes in v4:
time: 54.4 us; the launch traced here: 54.1 us
  starting transfers between devices  19.7 us (36%)
  Pallas kernels  14.7 us (27%)
  blocking collectives  12.9 us (24%)
  waiting for transfers between devices  6.68 us (12%)
    all_to_all x1, blocking collectives, exchange(): return lax.all_to_all(x, axes, 0, 0, tiled=True, axis_index_groups=groups)  12.9 us
    all_to_all x2, starting transfers between devices, exchange(): return lax.all_to_all(x, axes, 0, 0, tiled=True, axis_index_groups=groups)  12.2 us
    pallas_call x1, Pallas kernels, body(): call(factor_kernel, 'factor', [VMEM] * rows, shape((rank, 3 * rank), BF16...  5.75 us
    ppermute x1, starting transfers between devices, body(): other = lax.ppermute(first, 'rows', [(r, r ^ 1) for r in range(rows)])  5.63 us
    pallas_call x1, Pallas kernels, body(): call(mixed_kernel, 'mixed', [ANY, VMEM, VMEM], fast((slabs, pods, half, w...  4.83 us
    all_to_all x2, waiting for transfers between devices, exchange(): return lax.all_to_all(x, axes, 0, 0, tiled=True, axis_index_groups=groups)  4.79 us
    ppermute x3, starting transfers between devices, body(): lax.ppermute(normal, 'rows', [(r, r ^ n) for r in range(rows)])  1.94 us
    ppermute x3, waiting for transfers between devices, body(): lax.ppermute(normal, 'rows', [(r, r ^ n) for r in range(rows)])  1.89 us
  transfers between devices with their start and end apart: 6, of which 4 were waited for; matrix products, arithmetic and copies ran while one was open for 0% of the time, Pallas kernels for 22%

profile of v4, /device:TPU:8, one launch (start us, length us, event | category | flops | bytes accessed | tf_op | source)
XLA Modules:
  0.0 54.1 jit_solution(3585772547164584991)
XLA Ops:
  0.0 1.2 %first.1 = (f32[8,96,128]{2,1,0:T(8,128)S(1)}, f32[128,128]{1,0:T(8,128)S(1)}) custom-call(f32[64,256]{1,0:T(8,128)} %bitcast.6, f32[64,64]{1,0:T(8,128)} %c_ref.1), custom_call_target="tpu_custom_call" | custom-call | tf_op jit(solution)/shard_map/first/pallas_call | solution.py:227
  1.2 12.9 %all_to_all.15.own_ref.in_ref = f32[8,96,128]{2,1,0:T(8,128)S(1)} all-to-all(f32[8,96,128]{2,1,0:T(8,128)S(1)} %get-tuple-element.7), channel_id=1, replica_groups={{0,129,2,131,4,133,6,135},{8,137,10,139,12,141,14,143},{16,145,18,147,2..., dimensions={0} | all-to-all | bytes 786432 | tf_op jit(solution)/shard_map/all_to_all | solution.py:214
  14.1 5.6 %collective-permute-start = (f32[8,96,128]{2,1,0:T(8,128)S(1)}, f32[8,96,128]{2,1,0:T(8,128)S(1)}, u32[]{:S(2)}, u32[]{:S(2)}) collective-permute-start(f32[8,96,128]{2,1,0:T(8,128)S(1)} %all_to_all.15.own_ref.in_ref), channel_id=1, source_target_pairs={{0,64},{64,0},{128,192},{192,128},{1,65},{65,1},{129,193},{193,129... | collective-permute-start | bytes 1179656 | tf_op jit(solution)/shard_map/ppermute | solution.py:236
  19.8 1.2 %second.1 = f32[8,64,128]{2,1,0:T(8,128)} custom-call(f32[128,128]{1,0:T(8,128)S(1)} %get-tuple-element.8.b_ref, f32[8,96,128]{2,1,0:T(8,128)S(1)} %all_to_all.15.own_ref.in_ref), custom_call_target="tpu_custom_call" | custom-call | tf_op jit(solution)/shard_map/second/pallas_call | solution.py:237
  21.0 5.3 %all-to-all-start.1 = ((f32[8,64,128]{2,1,0:T(8,128)}), f32[8,64,128]{2,1,0:T(8,128)S(1)}, u32[]{:S(2)}, u32[]{:S(2)}) async-start(f32[8,64,128]{2,1,0:T(8,128)} %second.1), calls=%async_computation.1 | async-start | bytes 524288 | tf_op jit(solution)/shard_map/all_to_all | solution.py:214
  26.3 0.0 collective-permute-done.other_ref
  26.3 4.8 %mixed.1.mixed_ref = f32[2,8,128,128]{3,2,1,0:T(8,128)S(1)} custom-call(f32[2,2048,512]{2,1,0:T(8,128)} %t_ref.1, f32[8,96,128]{2,1,0:T(8,128)S(1)} %all_to_all.15.own_ref.in_ref, f32[8,96,128]{2,1,0:T(8,128)S(1)} %collective-permute-done.other_ref), custom_call_target="tpu_custom_call" | custom-call | flops 1073741824 | bytes 8388608 | tf_op jit(solution)/shard_map/mixed/pallas_call | solution.py:246
  31.2 2.4 %all-to-all-done.1.in_ref = f32[8,64,128]{2,1,0:T(8,128)S(1)} async-done(((f32[8,64,128]{2,1,0:T(8,128)}), f32[8,64,128]{2,1,0:T(8,128)S(1)}, u32[]{:S(2)}, u32[]{:S(2)}) %all-to-all-start.1) | async-done | bytes 262176 | tf_op jit(solution)/shard_map/all_to_all | solution.py:214
  33.6 0.8 %partial.1.partial_ref = f32[64,128]{1,0:T(8,128)} custom-call(f32[2,8,128,128]{3,2,1,0:T(8,128)S(1)} %mixed.1.mixed_ref, f32[8,96,128]{2,1,0:T(8,128)S(1)} %all_to_all.15.own_ref.in_ref, f32[8,96,128]{2,1,0:T(8,128)S(1)} %collective-permute-done.other_ref, f32[8,64,128]{2,1,0:T(8,128)S(1)} %all-to-all-done.1.in_ref), custom_call_target="tpu_custom_call" | custom-call | tf_op jit(solution)/shard_map/partial/pallas_call | solution.py:256
  34.4 6.8 %all-to-all-start.2 = ((f32[64,1,128]{2,1,0:T(1,128)}), f32[64,1,128]{2,1,0:T(1,128)S(1)}, u32[]{:S(2)}, u32[]{:S(2)}) async-start(f32[64,1,128]{2,1,0:T(1,128)} %bitcast.2), calls=%async_computation.2 | async-start | bytes 65536 | tf_op jit(solution)/shard_map/all_to_all | solution.py:214
  41.3 0.1 collective-permute-start.3
  41.4 1.2 %collective-permute-start.2 = (f32[16,128]{1,0:T(8,128)S(1)}, f32[16,128]{1,0:T(8,128)S(1)}, u32[]{:S(2)}, u32[]{:S(2)}) collective-permute-start(f32[16,128]{1,0:T(8,128)S(1)} %normal.1.refs_0_), channel_id=1, source_target_pairs={{0,128},{64,192},{128,0},{192,64},{1,129},{65,193},{129,1},{193,65... | collective-permute-start | bytes 24584 | tf_op jit(solution)/shard_map/ppermute | solution.py:267
  42.5 0.7 %collective-permute-start.1 = (f32[16,128]{1,0:T(8,128)S(1)}, f32[16,128]{1,0:T(8,128)S(1)}, u32[]{:S(2)}, u32[]{:S(2)}) collective-permute-start(f32[16,128]{1,0:T(8,128)S(1)} %normal.1.refs_0_), channel_id=1, source_target_pairs={{0,64},{64,0},{128,192},{192,128},{1,65},{65,1},{129,193},{193,129... | collective-permute-start | bytes 24584 | tf_op jit(solution)/shard_map/ppermute | solution.py:267
  43.2 1.2 %collective-permute-done.3.refs_3_ = f32[16,128]{1,0:T(8,128)S(1)} collective-permute-done((f32[16,128]{1,0:T(8,128)S(1)}, f32[16,128]{1,0:T(8,128)S(1)}, u32[]{:S(2)}, u32[]{:S(2)}) %collective-permute-start.3) | collective-permute-done | bytes 8224 | tf_op jit(solution)/shard_map/ppermute | solution.py:267
  44.4 0.7 %collective-permute-done.2.refs_2_ = f32[16,128]{1,0:T(8,128)S(1)} collective-permute-done((f32[16,128]{1,0:T(8,128)S(1)}, f32[16,128]{1,0:T(8,128)S(1)}, u32[]{:S(2)}, u32[]{:S(2)}) %collective-permute-start.2) | collective-permute-done | bytes 8224 | tf_op jit(solution)/shard_map/ppermute | solution.py:267
  45.1 0.0 collective-permute-done.1.refs_1_
  45.1 5.8 %factor.1.inverse_ref = bf16[64,192]{1,0:T(8,128)(2,1)S(1)} custom-call(f32[16,128]{1,0:T(8,128)S(1)} %normal.1.refs_0_, f32[16,128]{1,0:T(8,128)S(1)} %collective-permute-done.1.refs_1_, f32[16,128]{1,0:T(8,128)S(1)} %collective-permute-done.2.refs_2_, f32[16,128]{1,0:T(8,128)S(1)} %collective-permute-done.3.refs_3_), custom_call_target="tpu_custom_call" | custom-call | flops 1000000 | bytes 80000 | tf_op jit(solution)/shard_map/factor/pallas_call | solution.py:268
  50.9 2.3 %all-to-all-done.2 = f32[64,1,128]{2,1,0:T(1,128)S(1)} async-done(((f32[64,1,128]{2,1,0:T(1,128)}), f32[64,1,128]{2,1,0:T(1,128)S(1)}, u32[]{:S(2)}, u32[]{:S(2)}) %all-to-all-start.2) | async-done | bytes 32800 | tf_op jit(solution)/shard_map/all_to_all | solution.py:214
  53.2 0.8 %last.1 = f32[2,64]{1,0:T(2,128)} custom-call(f32[64,128]{1,0:T(8,128)S(1)} %bitcast.5, bf16[64,192]{1,0:T(8,128)(2,1)S(1)} %factor.1.inverse_ref), custom_call_target="tpu_custom_call" | custom-call | tf_op jit(solution)/shard_map/last/pallas_call | solution.py:276
  (1 shorter events, 0.0 us)
Async XLA Ops:
  14.1 12.2 %collective-permute-start = (f32[8,96,128]{2,1,0:T(8,128)S(1)}, f32[8,96,128]{2,1,0:T(8,128)S(1)}, u32[]{:S(2)}, u32[]{:S(2)}) collective-permute-start(f32[8,96,128]{2,1,0:T(8,128)S(1)} %all_to_all.15.own_ref.in_ref), channel_id=1, source_target_pairs={{0,64},{64,0},{128,192},{192,128},{1,65},{65,1},{129,193},{193,129... | collective-permute-start | bytes 1179656 | tf_op jit(solution)/shard_map/ppermute | solution.py:236
  21.0 12.6 %all-to-all-start.1 = ((f32[8,64,128]{2,1,0:T(8,128)}), f32[8,64,128]{2,1,0:T(8,128)S(1)}, u32[]{:S(2)}, u32[]{:S(2)}) async-start(f32[8,64,128]{2,1,0:T(8,128)} %second.1), calls=%async_computation.1 | async-start | bytes 524288 | tf_op jit(solution)/shard_map/all_to_all | solution.py:214
  34.4 18.8 %all-to-all-start.2 = ((f32[64,1,128]{2,1,0:T(1,128)}), f32[64,1,128]{2,1,0:T(1,128)S(1)}, u32[]{:S(2)}, u32[]{:S(2)}) async-start(f32[64,1,128]{2,1,0:T(1,128)} %bitcast.2), calls=%async_computation.2 | async-start | bytes 65536 | tf_op jit(solution)/shard_map/all_to_all | solution.py:214
  41.3 3.2 %collective-permute-start.3 = (f32[16,128]{1,0:T(8,128)S(1)}, f32[16,128]{1,0:T(8,128)S(1)}, u32[]{:S(2)}, u32[]{:S(2)}) collective-permute-start(f32[16,128]{1,0:T(8,128)S(1)} %normal.1.refs_0_), channel_id=1, source_target_pairs={{0,192},{64,128},{128,64},{192,0},{1,193},{65,129},{129,65},{193,1... | collective-permute-start | bytes 24584 | tf_op jit(solution)/shard_map/ppermute | solution.py:267
  41.4 3.7 %collective-permute-start.2 = (f32[16,128]{1,0:T(8,128)S(1)}, f32[16,128]{1,0:T(8,128)S(1)}, u32[]{:S(2)}, u32[]{:S(2)}) collective-permute-start(f32[16,128]{1,0:T(8,128)S(1)} %normal.1.refs_0_), channel_id=1, source_target_pairs={{0,128},{64,192},{128,0},{192,64},{1,129},{65,193},{129,1},{193,65... | collective-permute-start | bytes 24584 | tf_op jit(solution)/shard_map/ppermute | solution.py:267
  42.5 2.6 %collective-permute-start.1 = (f32[16,128]{1,0:T(8,128)S(1)}, f32[16,128]{1,0:T(8,128)S(1)}, u32[]{:S(2)}, u32[]{:S(2)}) collective-permute-start(f32[16,128]{1,0:T(8,128)S(1)} %normal.1.refs_0_), channel_id=1, source_target_pairs={{0,64},{64,0},{128,192},{192,128},{1,65},{65,1},{129,193},{193,129... | collective-permute-start | bytes 24584 | tf_op jit(solution)/shard_map/ppermute | solution.py:267

commit v5 on v4

v5 whole, which is shorter than its diff:
```python
import jax
import jax.numpy as jnp
from jax import lax
from jax.experimental import pallas as pl
from jax.experimental.pallas import tpu as pltpu
from jax.sharding import PartitionSpec as P

F32, BF16 = jnp.float32, jnp.bfloat16
HIGHEST = lax.Precision.HIGHEST
VMEM = pl.BlockSpec(memory_space=pltpu.VMEM)
ANY = pl.BlockSpec(memory_space=pl.ANY)
LIMIT = 24 * 1024 * 1024
ROWS, SLOTS = 1024, 3


def pieces(x, n):
    out = []
    for _ in range(n - 1):
        out.append(x.astype(BF16))
        x = x - out[-1].astype(F32)
    return out + [x.astype(BF16)]


def product(x, y, dim):
    (a, b, c), (d, e, f) = pieces(x, 3), pieces(y, 3)
    left = jnp.concatenate([a, a, a, b, b, c], axis=dim)
    right = jnp.concatenate([d, e, f, d, e, d], axis=dim)
    return lax.dot_general(left, right, (((dim,), (dim,)), ((), ())), preferred_element_type=F32)


def fold(x, axis=0):
    half = x.shape[axis] // 2
    index = [slice(None)] * x.ndim
    upper, lower = list(index), list(index)
    upper[axis], lower[axis] = slice(0, half), slice(half, None)
    return jnp.concatenate([x[tuple(upper)], x[tuple(lower)]], axis=-1)


def unfold(x):
    rank = x.shape[-1] // 2
    return jnp.concatenate([x[..., :rank], x[..., rank:]], axis=-2)


def gathers_b():
    return lax.axis_index("rows") % 2 == 0


def first_kernel(bt_ref, c_ref, out_ref, bt, c, sems):
    copies = [
        pltpu.make_async_copy(source, to, sems.at[n]) for n, (source, to) in enumerate(((bt_ref, bt), (c_ref, c)))
    ]
    for copy in copies:
        copy.start()
    for copy in copies:
        copy.wait()
    rows = out_ref.shape[1]

    def send(block):
        for n in range(out_ref.shape[0]):
            out_ref[n, : block.shape[0]] = block

    @pl.when(gathers_b())
    def _():
        send(jnp.concatenate([bt[:, :rows].T, bt[:, rows:].T], axis=1))

    @pl.when(jnp.logical_not(gathers_b()))
    def _():
        grams = [fold(product(bt[...], bt[...], 1)), fold(product(c[...], c[...], 0))]
        block = jnp.concatenate([fold(c[...]), *grams], axis=0)
        send(jnp.concatenate([block, jnp.zeros((rows - block.shape[0], block.shape[1]), F32)], axis=0))


def grams_kernel(in_ref, out_ref):
    rows = out_ref.shape[0]
    out_ref[...] = jnp.sum(in_ref[:, rows // 2 : rows // 2 + rows], axis=0)


def add_kernel(x_ref, y_ref, after_ref, out_ref):
    total = x_ref[...] + y_ref[...]
    rows = out_ref.shape[0]
    out_ref[...] = total if total.shape[0] == rows else total[:rows] * total[rows:]


def mixed_kernel(t_ref, own_ref, other_ref, out_ref, buffer, sems):
    slots, step, extent = buffer.shape
    devices, _, width = own_ref.shape
    rank = width // 2
    each = t_ref.shape[1] // step
    steps = t_ref.shape[0] * each

    def copy(n):
        at = pl.ds(pl.multiple_of(n % each * step, step), step)
        return pltpu.make_async_copy(t_ref.at[n // each, at], buffer.at[n % slots], sems.at[n % slots])

    for n in range(slots):
        copy(n).start()
    rows = extent // devices // 2
    c = jnp.where(gathers_b(), other_ref[:, :rows], own_ref[:, :rows])
    c = unfold(c).reshape(extent, rank)
    w = jnp.concatenate(pieces(c, 2), axis=1)
    half = out_ref.shape[2]
    left = lax.broadcasted_iota(jnp.int32, (half, width), 1) < rank

    def work(n, carry):
        copy(n).wait()
        high, low = pieces(buffer[n % slots], 2)
        both = jnp.dot(high, w, preferred_element_type=F32) + jnp.dot(low, w, preferred_element_type=F32)

        @pl.when(n + slots < steps)
        def _():
            copy(n + slots).start()

        both = both + pltpu.roll(both, rank, 1)
        for m in range(step // (2 * half)):
            part = both[2 * half * m : 2 * half * (m + 1)]
            out_ref[n // each, n % each * (step // (2 * half)) + m] = jnp.where(left, part[:half], part[half:])
        return carry

    lax.fori_loop(0, steps, work, 0)


def partial_kernel(mixed_ref, own_ref, other_ref, out_ref):
    half = mixed_ref.shape[2]
    width = mixed_ref.shape[3]
    mine = gathers_b()
    totals = [jnp.zeros((8, width), F32) for _ in range(2)]
    for n in range(mixed_ref.shape[1]):
        b = jnp.where(mine, own_ref[n], other_ref[n])
        for i in range(2):
            totals[i] = totals[i] + jnp.sum((mixed_ref[i, n] * b).reshape(half // 8, 8, width), axis=0)
    rows = []
    for total in totals:
        row = jnp.sum(total, axis=0, keepdims=True)
        rows.append(row + pltpu.roll(row, width // 2, 1))
    left = lax.broadcasted_iota(jnp.int32, (1, width), 1) < width // 2
    out_ref[...] = jnp.broadcast_to(jnp.where(left, rows[0], rows[1]), out_ref.shape)


def factor_kernel(own_ref, other_ref, out_ref, inverse):
    rank = inverse.shape[0]
    a = unfold(jnp.where(gathers_b(), other_ref[...], own_ref[...]))
    eye = lax.broadcasted_iota(jnp.int32, (rank, rank), 0) == lax.broadcasted_iota(jnp.int32, (rank, rank), 1)
    a = jnp.concatenate([a, eye.astype(F32)], axis=1)
    tile = 8
    tiles = [a[n : n + tile] for n in range(0, rank, tile)]

    def lanes(x, n):
        return jnp.broadcast_to(x[:, n : n + 1], x.shape)

    def sublanes(x, n):
        return jnp.broadcast_to(x[n : n + 1], x.shape)

    for t in range(len(tiles)):
        below = range(t, len(tiles))
        columns = {u: [lanes(tiles[u], tile * t + j) for j in range(tile)] for u in below}
        rows = [sublanes(tiles[t], j) for j in range(tile)]
        for j in range(tile):
            scale = lax.rsqrt(sublanes(columns[t][j], j))
            rows[j] = rows[j] * scale
            inverse[tile * t + j : tile * t + j + 1] = rows[j][:1, rank:]
            for u in below:
                columns[u][j] = columns[u][j] * scale
            for m in range(j + 1, tile):
                pivot = sublanes(columns[t][j], m)
                rows[m] = rows[m] - pivot * rows[j]
                for u in below:
                    columns[u][m] = columns[u][m] - columns[u][j] * pivot
        for u in below[1:]:
            for j in range(tile):
                tiles[u] = tiles[u] - columns[u][j] * rows[j]
    root = inverse[...]
    full = lax.dot_general(root, root, (((0,), (0,)), ((), ())), precision=HIGHEST, preferred_element_type=F32)
    out_ref[...] = jnp.concatenate(pieces(full, 3), axis=1)


def last_kernel(in_ref, inverse_ref, out_ref):
    rank = inverse_ref.shape[0]
    total = jnp.sum(in_ref[...], axis=0, keepdims=True)
    x = jnp.concatenate([total[:, :rank], total[:, rank:]], axis=0)
    parts = jnp.dot(jnp.concatenate(pieces(x, 3), axis=0), inverse_ref[...], preferred_element_type=F32)
    out_ref[...] = sum(
        parts[2 * n : 2 * n + 2, m * rank : (m + 1) * rank] for n in reversed(range(3)) for m in reversed(range(3 - n))
    )


def call(kernel, name, ins, outs, scratch=(), out=VMEM, **more):
    return pl.pallas_call(
        kernel,
        name=name,
        in_specs=ins,
        out_specs=out,
        out_shape=outs,
        scratch_shapes=scratch,
        compiler_params=pltpu.CompilerParams(vmem_limit_bytes=LIMIT),
        **more,
    )


def body(pairs, gather_groups, tensor, factor_b, factor_c):
    axes = ("rows", "racks", "pods")
    racks, pods = lax.axis_size("racks"), lax.axis_size("pods")
    slabs, _, extent_k = tensor.shape
    own_b, rank = factor_b.shape
    half, width = own_b // 2, 2 * rank
    shape, fast = jax.ShapeDtypeStruct, pltpu.VMEM
    tensor, bt, factor_c = (pltpu.with_memory_space_constraint(x, pltpu.HBM) for x in (tensor, factor_b.T, factor_c))
    small = pl.CostEstimate(flops=1_000_000, bytes_accessed=80_000, transcendentals=64)

    first = call(
        first_kernel,
        "first",
        [ANY, ANY],
        fast((racks, half, width), F32),
        [pltpu.VMEM(bt.shape, F32), pltpu.VMEM(factor_c.shape, F32), pltpu.SemaphoreType.DMA((2,))],
    )(bt, factor_c)
    first = lax.all_to_all(first, axes, 0, 0, tiled=True, axis_index_groups=gather_groups)
    chip = [(r, r ^ 1) for r in range(lax.axis_size("rows"))]
    other = lax.ppermute(first, "rows", chip)
    grams = call(grams_kernel, "grams", [VMEM], shape((rank, width), F32), cost_estimate=small)(first)
    mixed = call(
        mixed_kernel,
        "mixed",
        [ANY, VMEM, VMEM],
        fast((slabs, pods, half, width), F32),
        [pltpu.VMEM((SLOTS, ROWS, extent_k), F32), pltpu.SemaphoreType.DMA((SLOTS,))],
        cost_estimate=pl.CostEstimate(
            flops=4 * tensor.size * width, bytes_accessed=4 * tensor.size, transcendentals=0
        ),
    )(tensor, first, other)
    partial = call(partial_kernel, "partial", [VMEM] * 3, shape((racks * pods, width), F32))(mixed, first, other)
    for step, (pair, after) in enumerate(zip(pairs, (mixed, partial, partial), strict=True)):
        arrived = lax.ppermute(grams, axes, pair)
        rows = rank if step + 1 < len(pairs) else rank // 2
        grams = call(add_kernel, f"add{step}", [VMEM, VMEM, ANY], shape((rows, width), F32), cost_estimate=small)(
            grams, arrived, after
        )
    everyone = lax.all_to_all(partial.reshape(racks * pods, 1, width), ("racks", "pods"), 0, 0, tiled=True)
    inverse = call(
        factor_kernel,
        "factor",
        [VMEM] * 2,
        shape((rank, 3 * rank), BF16),
        [pltpu.VMEM((rank, rank), F32)],
        cost_estimate=small,
    )(grams, lax.ppermute(grams, "rows", chip))
    return call(last_kernel, "last", [VMEM, VMEM], shape((slabs, rank), F32))(
        everyone.reshape(racks * pods, width), inverse
    )


def routes(mesh):
    rows, racks, pods = (mesh.shape[axis] for axis in ("rows", "racks", "pods"))

    def device(low, core, z, p):
        return ((low * 2 + core) * racks + z) * pods + p

    every = [(low, z, p) for low in range(rows // 2) for z in range(racks) for p in range(pods)]
    pairs = [
        [(device(low, 1, z, p), device(to(low, p)[0], 1, z, to(low, p)[1])) for low, z, p in every]
        for to in (lambda low, p: (low ^ 1, p ^ 1), lambda low, p: (low, p ^ 2), lambda low, p: (low, p ^ 6))
    ]
    by_pods = [[device(low ^ (p % 2), 0, z, p) for p in range(pods)] for low in range(rows // 2) for z in range(racks)]
    by_racks = [[device(low, 1, z, p) for z in range(racks)] for low in range(rows // 2) for p in range(pods)]
    return pairs, by_pods + by_racks


def solution(mesh):
    pairs, groups = routes(mesh)

    def mapped(tensor, factor_b, factor_c):
        return body(pairs, groups, tensor, factor_b, factor_c)

    in_specs = (P("rows", "racks", "pods"), P(("racks", "pods"), None), P(("pods", "racks"), None))
    out_specs = P("rows", None)
    return jax.shard_map(mapped, mesh=mesh, in_specs=in_specs, out_specs=out_specs, check_vma=False)
```

time: 54.4 us -> 52.4 us (0.963)
  the two profiles are of different devices: /device:TPU:8 before, /device:TPU:1 now
where the time goes in v5:
time: 52.4 us; the launch traced here: 52.1 us
  blocking collectives  21 us (40%)
  starting transfers between devices  16.8 us (32%)
  Pallas kernels  9.84 us (19%)
  waiting for transfers between devices  4.38 us (8%)
    all_to_all x1, blocking collectives, body(): lax.all_to_all(first, axes, 0, 0, tiled=True, axis_index_groups=gather_gr...  21 us
    ppermute x3, starting transfers between devices, body(): arrived = lax.ppermute(grams, axes, pair)  11.9 us
    pallas_call x1, Pallas kernels, body(): call(mixed_kernel, 'mixed', [ANY, VMEM, VMEM], fast((slabs, pods, half, w...  4.82 us
    all_to_all x1, starting transfers between devices, body(): lax.all_to_all(partial.reshape(racks * pods, 1, width), ('racks', 'pods')...  4.81 us
    pallas_call x1, Pallas kernels, body(): call(factor_kernel, 'factor', [VMEM] * 2, shape((rank, 3 * rank), BF16),...  2.16 us
    ppermute x3, waiting for transfers between devices, body(): arrived = lax.ppermute(grams, axes, pair)  2.07 us
    ppermute x1, waiting for transfers between devices, body(): lax.ppermute(grams, 'rows', chip)  1.17 us
    pallas_call x1, Pallas kernels, body(): call(first_kernel, 'first', [ANY, ANY], fast((racks, half, width), F32),...  1.16 us
  transfers between devices with their start and end apart: 6, of which 3 were waited for; matrix products, arithmetic and copies ran while one was open for 0% of the time, Pallas kernels for 15%

profile of v5, /device:TPU:1, one launch (start us, length us, event | category | flops | bytes accessed | tf_op | source)
XLA Modules:
  0.0 52.1 jit_solution(16146099971746962326)
XLA Ops:
  0.0 1.2 %first.1 = f32[8,128,128]{2,1,0:T(8,128)S(1)} custom-call(f32[64,256]{1,0:T(8,128)} %bitcast.6, f32[64,64]{1,0:T(8,128)} %c_ref.1), custom_call_target="tpu_custom_call" | custom-call | tf_op jit(solution)/shard_map/first/pallas_call | solution.py:209
  1.2 21.0 %all_to_all.10.own_ref.in_ref = f32[8,128,128]{2,1,0:T(8,128)S(1)} all-to-all(f32[8,128,128]{2,1,0:T(8,128)S(1)} %first.1), channel_id=1, replica_groups={{0,129,2,131,4,133,6,135},{8,137,10,139,12,141,14,143},{16,145,18,147,2..., dimensions={0} | all-to-all | bytes 1048576 | tf_op jit(solution)/shard_map/all_to_all | solution.py:216
  22.1 0.0 collective-permute-start
  22.1 4.6 %collective-permute-start.1 = (f32[64,128]{1,0:T(8,128)S(1)}, f32[64,128]{1,0:T(8,128)S(1)}, u32[]{:S(2)}, u32[]{:S(2)}) collective-permute-start(f32[64,128]{1,0:T(8,128)S(1)} %grams.1.x_ref), channel_id=1, source_target_pairs={{64,193},{65,192},{66,195},{67,194},{68,197},{69,196},{70,199},{71... | collective-permute-start | bytes 98312 | tf_op jit(solution)/shard_map/ppermute | solution.py:232
  26.8 0.0 collective-permute-done.other_ref
  26.8 4.8 %mixed.1.mixed_ref.after_ref = f32[2,8,128,128]{3,2,1,0:T(8,128)S(1)} custom-call(f32[2,2048,512]{2,1,0:T(8,128)} %t_ref.1, f32[8,128,128]{2,1,0:T(8,128)S(1)} %all_to_all.10.own_ref.in_ref, f32[8,128,128]{2,1,0:T(8,128)S(1)} %collective-permute-done.other_ref), custom_call_target="tpu_custom_call" | custom-call | flops 1073741824 | bytes 8388608 | tf_op jit(solution)/shard_map/mixed/pallas_call | solution.py:220
  31.6 0.0 collective-permute-done.1.y_ref
  31.7 3.1 %collective-permute-start.2 = (f32[64,128]{1,0:T(8,128)S(1)}, f32[64,128]{1,0:T(8,128)S(1)}, u32[]{:S(2)}, u32[]{:S(2)}) collective-permute-start(f32[64,128]{1,0:T(8,128)S(1)} %add0.1.x_ref), channel_id=1, source_target_pairs={{64,66},{65,67},{66,64},{67,65},{68,70},{69,71},{70,68},{71,69},{7... | collective-permute-start | bytes 98312 | tf_op jit(solution)/shard_map/ppermute | solution.py:232
  34.8 0.8 %partial.1.after_ref = f32[64,128]{1,0:T(8,128)} custom-call(f32[2,8,128,128]{3,2,1,0:T(8,128)S(1)} %mixed.1.mixed_ref.after_ref, f32[8,128,128]{2,1,0:T(8,128)S(1)} %all_to_all.10.own_ref.in_ref, f32[8,128,128]{2,1,0:T(8,128)S(1)} %collective-permute-done.other_ref), custom_call_target="tpu_custom_call" | custom-call | tf_op jit(solution)/shard_map/partial/pallas_call | solution.py:230
  35.6 4.8 %all-to-all-start.1 = ((f32[64,1,128]{2,1,0:T(1,128)}), f32[64,1,128]{2,1,0:T(1,128)S(1)}, u32[]{:S(2)}, u32[]{:S(2)}) async-start(f32[64,1,128]{2,1,0:T(1,128)} %bitcast.2), calls=%async_computation.1 | async-start | bytes 65536 | tf_op jit(solution)/shard_map/all_to_all | solution.py:237
  40.4 0.0 collective-permute-done.2.y_ref
  40.5 4.1 %collective-permute-start.3 = (f32[64,128]{1,0:T(8,128)S(1)}, f32[64,128]{1,0:T(8,128)S(1)}, u32[]{:S(2)}, u32[]{:S(2)}) collective-permute-start(f32[64,128]{1,0:T(8,128)S(1)} %add1.1.x_ref), channel_id=1, source_target_pairs={{64,70},{65,71},{66,68},{67,69},{68,66},{69,67},{70,64},{71,65},{7... | collective-permute-start | bytes 98312 | tf_op jit(solution)/shard_map/ppermute | solution.py:232
  44.6 2.1 %collective-permute-done.3.y_ref = f32[64,128]{1,0:T(8,128)S(1)} collective-permute-done((f32[64,128]{1,0:T(8,128)S(1)}, f32[64,128]{1,0:T(8,128)S(1)}, u32[]{:S(2)}, u32[]{:S(2)}) %collective-permute-start.3) | collective-permute-done | bytes 32800 | tf_op jit(solution)/shard_map/ppermute | solution.py:232
  46.7 0.1 collective-permute-start.4
  46.8 1.2 %collective-permute-done.4.other_ref = f32[32,128]{1,0:T(8,128)S(1)} collective-permute-done((f32[32,128]{1,0:T(8,128)S(1)}, f32[32,128]{1,0:T(8,128)S(1)}, u32[]{:S(2)}, u32[]{:S(2)}) %collective-permute-start.4) | collective-permute-done | bytes 16416 | tf_op jit(solution)/shard_map/ppermute | solution.py:245
  47.9 2.2 %factor.1.inverse_ref = bf16[64,192]{1,0:T(8,128)(2,1)S(1)} custom-call(f32[32,128]{1,0:T(8,128)S(1)} %add2.1.own_ref, f32[32,128]{1,0:T(8,128)S(1)} %collective-permute-done.4.other_ref), custom_call_target="tpu_custom_call" | custom-call | flops 1000000 | bytes 80000 | tf_op jit(solution)/shard_map/factor/pallas_call | solution.py:238
  50.1 1.1 %all-to-all-done.1 = f32[64,1,128]{2,1,0:T(1,128)S(1)} async-done(((f32[64,1,128]{2,1,0:T(1,128)}), f32[64,1,128]{2,1,0:T(1,128)S(1)}, u32[]{:S(2)}, u32[]{:S(2)}) %all-to-all-start.1) | async-done | bytes 32800 | tf_op jit(solution)/shard_map/all_to_all | solution.py:237
  51.2 0.8 %last.1 = f32[2,64]{1,0:T(2,128)} custom-call(f32[64,128]{1,0:T(8,128)S(1)} %bitcast.5, bf16[64,192]{1,0:T(8,128)(2,1)S(1)} %factor.1.inverse_ref), custom_call_target="tpu_custom_call" | custom-call | tf_op jit(solution)/shard_map/last/pallas_call | solution.py:246
  (4 shorter events, 0.0 us)
Async XLA Ops:
  22.1 4.7 %collective-permute-start = (f32[8,128,128]{2,1,0:T(8,128)S(1)}, f32[8,128,128]{2,1,0:T(8,128)S(1)}, u32[]{:S(2)}, u32[]{:S(2)}) collective-permute-start(f32[8,128,128]{2,1,0:T(8,128)S(1)} %all_to_all.10.own_ref.in_ref), channel_id=1, source_target_pairs={{0,64},{64,0},{128,192},{192,128},{1,65},{65,1},{129,193},{193,129... | collective-permute-start | bytes 1572872 | tf_op jit(solution)/shard_map/ppermute | solution.py:218
  22.1 9.5 %collective-permute-start.1 = (f32[64,128]{1,0:T(8,128)S(1)}, f32[64,128]{1,0:T(8,128)S(1)}, u32[]{:S(2)}, u32[]{:S(2)}) collective-permute-start(f32[64,128]{1,0:T(8,128)S(1)} %grams.1.x_ref), channel_id=1, source_target_pairs={{64,193},{65,192},{66,195},{67,194},{68,197},{69,196},{70,199},{71... | collective-permute-start | bytes 98312 | tf_op jit(solution)/shard_map/ppermute | solution.py:232
  31.7 8.8 %collective-permute-start.2 = (f32[64,128]{1,0:T(8,128)S(1)}, f32[64,128]{1,0:T(8,128)S(1)}, u32[]{:S(2)}, u32[]{:S(2)}) collective-permute-start(f32[64,128]{1,0:T(8,128)S(1)} %add0.1.x_ref), channel_id=1, source_target_pairs={{64,66},{65,67},{66,64},{67,65},{68,70},{69,71},{70,68},{71,69},{7... | collective-permute-start | bytes 98312 | tf_op jit(solution)/shard_map/ppermute | solution.py:232
  35.6 15.6 %all-to-all-start.1 = ((f32[64,1,128]{2,1,0:T(1,128)}), f32[64,1,128]{2,1,0:T(1,128)S(1)}, u32[]{:S(2)}, u32[]{:S(2)}) async-start(f32[64,1,128]{2,1,0:T(1,128)} %bitcast.2), calls=%async_computation.1 | async-start | bytes 65536 | tf_op jit(solution)/shard_map/all_to_all | solution.py:237
  40.5 6.2 %collective-permute-start.3 = (f32[64,128]{1,0:T(8,128)S(1)}, f32[64,128]{1,0:T(8,128)S(1)}, u32[]{:S(2)}, u32[]{:S(2)}) collective-permute-start(f32[64,128]{1,0:T(8,128)S(1)} %add1.1.x_ref), channel_id=1, source_target_pairs={{64,70},{65,71},{66,68},{67,69},{68,66},{69,67},{70,64},{71,65},{7... | collective-permute-start | bytes 98312 | tf_op jit(solution)/shard_map/ppermute | solution.py:232
  46.7 1.3 %collective-permute-start.4 = (f32[32,128]{1,0:T(8,128)S(1)}, f32[32,128]{1,0:T(8,128)S(1)}, u32[]{:S(2)}, u32[]{:S(2)}) collective-permute-start(f32[32,128]{1,0:T(8,128)S(1)} %add2.1.own_ref), channel_id=1, source_target_pairs={{0,64},{64,0},{128,192},{192,128},{1,65},{65,1},{129,193},{193,129... | collective-permute-start | bytes 49160 | tf_op jit(solution)/shard_map/ppermute | solution.py:245

commit v6 on v5

--- a/solution.py
+++ b/solution.py
@@ -70,15 +70,14 @@
         send(jnp.concatenate([block, jnp.zeros((rows - block.shape[0], block.shape[1]), F32)], axis=0))
 
 
-def grams_kernel(in_ref, out_ref):
+def grams_kernel(own_ref, other_ref, out_ref):
     rows = out_ref.shape[0]
-    out_ref[...] = jnp.sum(in_ref[:, rows // 2 : rows // 2 + rows], axis=0)
+    at = slice(rows // 2, rows // 2 + rows)
+    out_ref[...] = jnp.sum(jnp.where(gathers_b(), other_ref[:, at], own_ref[:, at]), axis=0)
 
 
 def add_kernel(x_ref, y_ref, after_ref, out_ref):
-    total = x_ref[...] + y_ref[...]
-    rows = out_ref.shape[0]
-    out_ref[...] = total if total.shape[0] == rows else total[:rows] * total[rows:]
+    out_ref[...] = x_ref[...] + y_ref[...]
 
 
 def mixed_kernel(t_ref, own_ref, other_ref, out_ref, buffer, sems):
@@ -136,9 +135,15 @@
     out_ref[...] = jnp.broadcast_to(jnp.where(left, rows[0], rows[1]), out_ref.shape)
 
 
-def factor_kernel(own_ref, other_ref, out_ref, inverse):
+def factor_kernel(*refs):
+    parts, out_ref, (grams, inverse) = refs[:-3], refs[-3], refs[-2:]
     rank = inverse.shape[0]
-    a = unfold(jnp.where(gathers_b(), other_ref[...], own_ref[...]))
+    for n, part in enumerate(parts):
+        grams[jnp.bitwise_xor(lax.axis_index("pods") // 2, n)] = part[...]
+    both = grams[0]
+    for n in range(1, len(parts)):
+        both = both + grams[n]
+    a = unfold(both[: rank // 2] * both[rank // 2 :])
     eye = lax.broadcasted_iota(jnp.int32, (rank, rank), 0) == lax.broadcasted_iota(jnp.int32, (rank, rank), 1)
     a = jnp.concatenate([a, eye.astype(F32)], axis=1)
     tile = 8
@@ -214,9 +219,9 @@
         [pltpu.VMEM(bt.shape, F32), pltpu.VMEM(factor_c.shape, F32), pltpu.SemaphoreType.DMA((2,))],
     )(bt, factor_c)
     first = lax.all_to_all(first, axes, 0, 0, tiled=True, axis_index_groups=gather_groups)
-    chip = [(r, r ^ 1) for r in range(lax.axis_size("rows"))]
-    other = lax.ppermute(first, "rows", chip)
-    grams = call(grams_kernel, "grams", [VMEM], shape((rank, width), F32), cost_estimate=small)(first)
+    other = lax.ppermute(first, "rows", [(r, r ^ 1) for r in range(lax.axis_size("rows"))])
+    grams = call(grams_kernel, "grams", [VMEM] * 2, shape((rank, width), F32), cost_estimate=small)(first, other)
+    arrived = lax.ppermute(grams, axes, pairs)
     mixed = call(
         mixed_kernel,
         "mixed",
@@ -228,21 +233,19 @@
         ),
     )(tensor, first, other)
     partial = call(partial_kernel, "partial", [VMEM] * 3, shape((racks * pods, width), F32))(mixed, first, other)
-    for step, (pair, after) in enumerate(zip(pairs, (mixed, partial, partial), strict=True)):
-        arrived = lax.ppermute(grams, axes, pair)
-        rows = rank if step + 1 < len(pairs) else rank // 2
-        grams = call(add_kernel, f"add{step}", [VMEM, VMEM, ANY], shape((rows, width), F32), cost_estimate=small)(
-            grams, arrived, after
-        )
+    grams = call(add_kernel, "add", [VMEM, VMEM, ANY], shape((rank, width), F32), cost_estimate=small)(
+        grams, arrived, partial
+    )
+    parts = [grams] + [lax.ppermute(grams, "pods", [(p, p ^ n) for p in range(pods)]) for n in range(2, pods, 2)]
     everyone = lax.all_to_all(partial.reshape(racks * pods, 1, width), ("racks", "pods"), 0, 0, tiled=True)
     inverse = call(
         factor_kernel,
         "factor",
-        [VMEM] * 2,
+        [VMEM] * len(parts),
         shape((rank, 3 * rank), BF16),
-        [pltpu.VMEM((rank, rank), F32)],
+        [pltpu.VMEM((len(parts), rank, width), F32), pltpu.VMEM((rank, rank), F32)],
         cost_estimate=small,
-    )(grams, lax.ppermute(grams, "rows", chip))
+    )(*parts)
     return call(last_kernel, "last", [VMEM, VMEM], shape((slabs, rank), F32))(
         everyone.reshape(racks * pods, width), inverse
     )
@@ -254,10 +257,12 @@
     def device(low, core, z, p):
         return ((low * 2 + core) * racks + z) * pods + p
 
-    every = [(low, z, p) for low in range(rows // 2) for z in range(racks) for p in range(pods)]
     pairs = [
-        [(device(low, 1, z, p), device(to(low, p)[0], 1, z, to(low, p)[1])) for low, z, p in every]
-        for to in (lambda low, p: (low ^ 1, p ^ 1), lambda low, p: (low, p ^ 2), lambda low, p: (low, p ^ 6))
+        (device(low, core, z, p), device(low ^ 1, core, z, p ^ 1))
+        for low in range(rows // 2)
+        for core in range(2)
+        for z in range(racks)
+        for p in range(pods)
     ]
     by_pods = [[device(low ^ (p % 2), 0, z, p) for p in range(pods)] for low in range(rows // 2) for z in range(racks)]
     by_racks = [[device(low, 1, z, p) for z in range(racks)] for low in range(rows // 2) for p in range(pods)]

time: 52.4 us -> 50.5 us (0.964)
  the two profiles are of different devices: /device:TPU:1 before, /device:TPU:8 now
where the time goes in v6:
time: 50.5 us; the launch traced here: 50 us
  starting transfers between devices  20.2 us (40%)
  blocking collectives  13.4 us (27%)
  Pallas kernels  9.71 us (19%)
  waiting for transfers between devices  6.55 us (13%)
    all_to_all x1, blocking collectives, body(): lax.all_to_all(first, axes, 0, 0, tiled=True, axis_index_groups=gather_gr...  13.4 us
    all_to_all x1, starting transfers between devices, body(): lax.all_to_all(partial.reshape(racks * pods, 1, width), ('racks', 'pods')...  7.1 us
    ppermute x1, starting transfers between devices, body(): lax.ppermute(first, 'rows', [(r, r ^ 1) for r in range(lax.axis_size('row...  6.65 us
    pallas_call x1, Pallas kernels, body(): call(mixed_kernel, 'mixed', [ANY, VMEM, VMEM], fast((slabs, pods, half, w...  4.82 us
    ppermute x3, starting transfers between devices, body(): lax.ppermute(grams, 'pods', [(p, p ^ n) for p in range(pods)])  4.79 us
    ppermute x3, waiting for transfers between devices, body(): lax.ppermute(grams, 'pods', [(p, p ^ n) for p in range(pods)])  4.68 us
    pallas_call x1, Pallas kernels, body(): call(factor_kernel, 'factor', [VMEM] * len(parts), shape((rank, 3 * rank)...  2.16 us
    ppermute x1, starting transfers between devices, body(): arrived = lax.ppermute(grams, axes, pairs)  1.68 us
  transfers between devices with their start and end apart: 6, of which 4 were waited for; matrix products, arithmetic and copies ran while one was open for 0% of the time, Pallas kernels for 16%

profile of v6, /device:TPU:8, one launch (start us, length us, event | category | flops | bytes accessed | tf_op | source)
XLA Modules:
  0.0 50.0 jit_solution(2858858824104408006)
XLA Ops:
  0.0 1.0 %first.1 = f32[8,128,128]{2,1,0:T(8,128)S(1)} custom-call(f32[64,256]{1,0:T(8,128)} %bitcast.6, f32[64,64]{1,0:T(8,128)} %c_ref.1), custom_call_target="tpu_custom_call" | custom-call | tf_op jit(solution)/shard_map/first/pallas_call | solution.py:214
  1.0 13.4 %all_to_all.10.own_ref = f32[8,128,128]{2,1,0:T(8,128)S(1)} all-to-all(f32[8,128,128]{2,1,0:T(8,128)S(1)} %first.1), channel_id=1, replica_groups={{0,129,2,131,4,133,6,135},{8,137,10,139,12,141,14,143},{16,145,18,147,2..., dimensions={0} | all-to-all | bytes 1048576 | tf_op jit(solution)/shard_map/all_to_all | solution.py:221
  14.5 6.6 %collective-permute-start = (f32[8,128,128]{2,1,0:T(8,128)S(1)}, f32[8,128,128]{2,1,0:T(8,128)S(1)}, u32[]{:S(2)}, u32[]{:S(2)}) collective-permute-start(f32[8,128,128]{2,1,0:T(8,128)S(1)} %all_to_all.10.own_ref), channel_id=1, source_target_pairs={{0,64},{64,0},{128,192},{192,128},{1,65},{65,1},{129,193},{193,129... | collective-permute-start | bytes 1572872 | tf_op jit(solution)/shard_map/ppermute | solution.py:222
  21.1 1.5 %collective-permute-done.other_ref = f32[8,128,128]{2,1,0:T(8,128)S(1)} collective-permute-done((f32[8,128,128]{2,1,0:T(8,128)S(1)}, f32[8,128,128]{2,1,0:T(8,128)S(1)}, u32[]{:S(2)}, u32[]{:S(2)}) %collective-permute-start) | collective-permute-done | bytes 524320 | tf_op jit(solution)/shard_map/ppermute | solution.py:222
  22.7 1.7 %collective-permute-start.1 = (f32[64,128]{1,0:T(8,128)S(1)}, f32[64,128]{1,0:T(8,128)S(1)}, u32[]{:S(2)}, u32[]{:S(2)}) collective-permute-start(f32[64,128]{1,0:T(8,128)S(1)} %grams.1.x_ref), channel_id=1, source_target_pairs={{0,129},{1,128},{2,131},{3,130},{4,133},{5,132},{6,135},{7,134},{8... | collective-permute-start | bytes 98312 | tf_op jit(solution)/shard_map/ppermute | solution.py:224
  24.4 4.8 %mixed.1.mixed_ref = f32[2,8,128,128]{3,2,1,0:T(8,128)S(1)} custom-call(f32[2,2048,512]{2,1,0:T(8,128)} %t_ref.1, f32[8,128,128]{2,1,0:T(8,128)S(1)} %all_to_all.10.own_ref, f32[8,128,128]{2,1,0:T(8,128)S(1)} %collective-permute-done.other_ref), custom_call_target="tpu_custom_call" | custom-call | flops 1073741824 | bytes 8388608 | tf_op jit(solution)/shard_map/mixed/pallas_call | solution.py:225
  29.2 0.8 %partial.1.after_ref = f32[64,128]{1,0:T(8,128)} custom-call(f32[2,8,128,128]{3,2,1,0:T(8,128)S(1)} %mixed.1.mixed_ref, f32[8,128,128]{2,1,0:T(8,128)S(1)} %all_to_all.10.own_ref, f32[8,128,128]{2,1,0:T(8,128)S(1)} %collective-permute-done.other_ref), custom_call_target="tpu_custom_call" | custom-call | tf_op jit(solution)/shard_map/partial/pallas_call | solution.py:235
  30.0 7.1 %all-to-all-start.1 = ((f32[64,1,128]{2,1,0:T(1,128)}), f32[64,1,128]{2,1,0:T(1,128)S(1)}, u32[]{:S(2)}, u32[]{:S(2)}) async-start(f32[64,1,128]{2,1,0:T(1,128)} %bitcast.2), calls=%async_computation.1 | async-start | bytes 65536 | tf_op jit(solution)/shard_map/all_to_all | solution.py:240
  37.1 0.0 collective-permute-done.1.y_ref
  37.2 1.7 %collective-permute-start.2 = (f32[64,128]{1,0:T(8,128)S(1)}, f32[64,128]{1,0:T(8,128)S(1)}, u32[]{:S(2)}, u32[]{:S(2)}) collective-permute-start(f32[64,128]{1,0:T(8,128)S(1)} %add.1.refs_0_), channel_id=1, source_target_pairs={{0,2},{1,3},{2,0},{3,1},{4,6},{5,7},{6,4},{7,5},{8,10},{9,11},{10,... | collective-permute-start | bytes 98312 | tf_op jit(solution)/shard_map/ppermute | solution.py:239
  38.8 2.7 %collective-permute-start.3 = (f32[64,128]{1,0:T(8,128)S(1)}, f32[64,128]{1,0:T(8,128)S(1)}, u32[]{:S(2)}, u32[]{:S(2)}) collective-permute-start(f32[64,128]{1,0:T(8,128)S(1)} %add.1.refs_0_), channel_id=1, source_target_pairs={{0,4},{1,5},{2,6},{3,7},{4,0},{5,1},{6,2},{7,3},{8,12},{9,13},{10,... | collective-permute-start | bytes 98312 | tf_op jit(solution)/shard_map/ppermute | solution.py:239
  41.5 0.5 collective-permute-start.4
  42.0 0.0 collective-permute-done.2.refs_1_
  42.0 2.4 %collective-permute-done.3.refs_2_ = f32[64,128]{1,0:T(8,128)S(1)} collective-permute-done((f32[64,128]{1,0:T(8,128)S(1)}, f32[64,128]{1,0:T(8,128)S(1)}, u32[]{:S(2)}, u32[]{:S(2)}) %collective-permute-start.3) | collective-permute-done | bytes 32800 | tf_op jit(solution)/shard_map/ppermute | solution.py:239
  44.4 2.3 %collective-permute-done.4.refs_3_ = f32[64,128]{1,0:T(8,128)S(1)} collective-permute-done((f32[64,128]{1,0:T(8,128)S(1)}, f32[64,128]{1,0:T(8,128)S(1)}, u32[]{:S(2)}, u32[]{:S(2)}) %collective-permute-start.4) | collective-permute-done | bytes 32800 | tf_op jit(solution)/shard_map/ppermute | solution.py:239
  46.6 2.2 %factor.1.inverse_ref = bf16[64,192]{1,0:T(8,128)(2,1)S(1)} custom-call(f32[64,128]{1,0:T(8,128)S(1)} %add.1.refs_0_, f32[64,128]{1,0:T(8,128)S(1)} %collective-permute-done.2.refs_1_, f32[64,128]{1,0:T(8,128)S(1)} %collective-permute-done.3.refs_2_, f32[64,128]{1,0:T(8,128)S(1)} %collective-permute-done.4.refs_3_), custom_call_target="tpu_custom_call" | custom-call | flops 1000000 | bytes 80000 | tf_op jit(solution)/shard_map/factor/pallas_call | solution.py:241
  48.8 0.3 all-to-all-done.1
  49.1 0.8 %last.1 = f32[2,64]{1,0:T(2,128)} custom-call(f32[64,128]{1,0:T(8,128)S(1)} %bitcast.5, bf16[64,192]{1,0:T(8,128)(2,1)S(1)} %factor.1.inverse_ref), custom_call_target="tpu_custom_call" | custom-call | tf_op jit(solution)/shard_map/last/pallas_call | solution.py:249
  (2 shorter events, 0.0 us)
Async XLA Ops:
  14.5 8.2 %collective-permute-start = (f32[8,128,128]{2,1,0:T(8,128)S(1)}, f32[8,128,128]{2,1,0:T(8,128)S(1)}, u32[]{:S(2)}, u32[]{:S(2)}) collective-permute-start(f32[8,128,128]{2,1,0:T(8,128)S(1)} %all_to_all.10.own_ref), channel_id=1, source_target_pairs={{0,64},{64,0},{128,192},{192,128},{1,65},{65,1},{129,193},{193,129... | collective-permute-start | bytes 1572872 | tf_op jit(solution)/shard_map/ppermute | solution.py:222
  22.7 14.4 %collective-permute-start.1 = (f32[64,128]{1,0:T(8,128)S(1)}, f32[64,128]{1,0:T(8,128)S(1)}, u32[]{:S(2)}, u32[]{:S(2)}) collective-permute-start(f32[64,128]{1,0:T(8,128)S(1)} %grams.1.x_ref), channel_id=1, source_target_pairs={{0,129},{1,128},{2,131},{3,130},{4,133},{5,132},{6,135},{7,134},{8... | collective-permute-start | bytes 98312 | tf_op jit(solution)/shard_map/ppermute | solution.py:224
  30.0 19.1 %all-to-all-start.1 = ((f32[64,1,128]{2,1,0:T(1,128)}), f32[64,1,128]{2,1,0:T(1,128)S(1)}, u32[]{:S(2)}, u32[]{:S(2)}) async-start(f32[64,1,128]{2,1,0:T(1,128)} %bitcast.2), calls=%async_computation.1 | async-start | bytes 65536 | tf_op jit(solution)/shard_map/all_to_all | solution.py:240
  37.2 4.8 %collective-permute-start.2 = (f32[64,128]{1,0:T(8,128)S(1)}, f32[64,128]{1,0:T(8,128)S(1)}, u32[]{:S(2)}, u32[]{:S(2)}) collective-permute-start(f32[64,128]{1,0:T(8,128)S(1)} %add.1.refs_0_), channel_id=1, source_target_pairs={{0,2},{1,3},{2,0},{3,1},{4,6},{5,7},{6,4},{7,5},{8,10},{9,11},{10,... | collective-permute-start | bytes 98312 | tf_op jit(solution)/shard_map/ppermute | solution.py:239
  38.8 5.5 %collective-permute-start.3 = (f32[64,128]{1,0:T(8,128)S(1)}, f32[64,128]{1,0:T(8,128)S(1)}, u32[]{:S(2)}, u32[]{:S(2)}) collective-permute-start(f32[64,128]{1,0:T(8,128)S(1)} %add.1.refs_0_), channel_id=1, source_target_pairs={{0,4},{1,5},{2,6},{3,7},{4,0},{5,1},{6,2},{7,3},{8,12},{9,13},{10,... | collective-permute-start | bytes 98312 | tf_op jit(solution)/shard_map/ppermute | solution.py:239
  41.5 5.1 %collective-permute-start.4 = (f32[64,128]{1,0:T(8,128)S(1)}, f32[64,128]{1,0:T(8,128)S(1)}, u32[]{:S(2)}, u32[]{:S(2)}) collective-permute-start(f32[64,128]{1,0:T(8,128)S(1)} %add.1.refs_0_), channel_id=1, source_target_pairs={{0,6},{1,7},{2,4},{3,5},{4,2},{5,3},{6,0},{7,1},{8,14},{9,15},{10,... | collective-permute-start | bytes 98312 | tf_op jit(solution)/shard_map/ppermute | solution.py:239

commit v7 on v6

--- a/solution.py
+++ b/solution.py
@@ -10,7 +10,7 @@
 VMEM = pl.BlockSpec(memory_space=pltpu.VMEM)
 ANY = pl.BlockSpec(memory_space=pl.ANY)
 LIMIT = 24 * 1024 * 1024
-ROWS, SLOTS = 1024, 3
+ROWS = 512
 
 
 def pieces(x, n):
@@ -80,42 +80,36 @@
     out_ref[...] = x_ref[...] + y_ref[...]
 
 
-def mixed_kernel(t_ref, own_ref, other_ref, out_ref, buffer, sems):
-    slots, step, extent = buffer.shape
+def load_kernel(t_ref, after_ref, out_ref, sems):
+    rows = out_ref.shape[1] // (sems.shape[0] // 2)
+    copies = []
+    for n in range(sems.shape[0]):
+        i, j = n % 2, n // 2 * rows
+        copies.append(
+            pltpu.make_async_copy(t_ref.at[i, pl.ds(j, rows)], out_ref.at[i, pl.ds(j, rows)], sems.at[n])
+        )
+        copies[-1].start()
+    for copy in copies:
+        copy.wait()
+
+
+def mixed_kernel(t_ref, own_ref, other_ref, out_ref):
     devices, _, width = own_ref.shape
+    half = out_ref.shape[2]
     rank = width // 2
-    each = t_ref.shape[1] // step
-    steps = t_ref.shape[0] * each
-
-    def copy(n):
-        at = pl.ds(pl.multiple_of(n % each * step, step), step)
-        return pltpu.make_async_copy(t_ref.at[n // each, at], buffer.at[n % slots], sems.at[n % slots])
-
-    for n in range(slots):
-        copy(n).start()
+    slabs, extent_j, extent = t_ref.shape
     rows = extent // devices // 2
     c = jnp.where(gathers_b(), other_ref[:, :rows], own_ref[:, :rows])
-    c = unfold(c).reshape(extent, rank)
-    w = jnp.concatenate(pieces(c, 2), axis=1)
-    half = out_ref.shape[2]
+    w = jnp.concatenate(pieces(unfold(c).reshape(extent, rank), 2), axis=1)
     left = lax.broadcasted_iota(jnp.int32, (half, width), 1) < rank
-
-    def work(n, carry):
-        copy(n).wait()
-        high, low = pieces(buffer[n % slots], 2)
-        both = jnp.dot(high, w, preferred_element_type=F32) + jnp.dot(low, w, preferred_element_type=F32)
-
-        @pl.when(n + slots < steps)
-        def _():
-            copy(n + slots).start()
-
-        both = both + pltpu.roll(both, rank, 1)
-        for m in range(step // (2 * half)):
-            part = both[2 * half * m : 2 * half * (m + 1)]
-            out_ref[n // each, n % each * (step // (2 * half)) + m] = jnp.where(left, part[:half], part[half:])
-        return carry
-
-    lax.fori_loop(0, steps, work, 0)
+    for i in range(slabs):
+        for n in range(0, extent_j, ROWS):
+            high, low = pieces(t_ref[i, n : n + ROWS], 2)
+            both = jnp.dot(high, w, preferred_element_type=F32) + jnp.dot(low, w, preferred_element_type=F32)
+            both = both + pltpu.roll(both, rank, 1)
+            for m in range(0, ROWS, 2 * half):
+                part = both[m : m + 2 * half]
+                out_ref[i, (n + m) // (2 * half)] = jnp.where(left, part[:half], part[half:])
 
 
 def partial_kernel(mixed_ref, own_ref, other_ref, out_ref):
@@ -204,7 +198,7 @@
 def body(pairs, gather_groups, tensor, factor_b, factor_c):
     axes = ("rows", "racks", "pods")
     racks, pods = lax.axis_size("racks"), lax.axis_size("pods")
-    slabs, _, extent_k = tensor.shape
+    slabs = tensor.shape[0]
     own_b, rank = factor_b.shape
     half, width = own_b // 2, 2 * rank
     shape, fast = jax.ShapeDtypeStruct, pltpu.VMEM
@@ -222,16 +216,23 @@
     other = lax.ppermute(first, "rows", [(r, r ^ 1) for r in range(lax.axis_size("rows"))])
     grams = call(grams_kernel, "grams", [VMEM] * 2, shape((rank, width), F32), cost_estimate=small)(first, other)
     arrived = lax.ppermute(grams, axes, pairs)
+    loaded = call(
+        load_kernel,
+        "load",
+        [ANY, ANY],
+        fast(tensor.shape, F32),
+        [pltpu.SemaphoreType.DMA((8,))],
+        cost_estimate=pl.CostEstimate(flops=0, bytes_accessed=4 * tensor.size, transcendentals=0),
+    )(tensor, first)
     mixed = call(
         mixed_kernel,
         "mixed",
-        [ANY, VMEM, VMEM],
+        [VMEM] * 3,
         fast((slabs, pods, half, width), F32),
-        [pltpu.VMEM((SLOTS, ROWS, extent_k), F32), pltpu.SemaphoreType.DMA((SLOTS,))],
         cost_estimate=pl.CostEstimate(
             flops=4 * tensor.size * width, bytes_accessed=4 * tensor.size, transcendentals=0
         ),
-    )(tensor, first, other)
+    )(loaded, first, other)
     partial = call(partial_kernel, "partial", [VMEM] * 3, shape((racks * pods, width), F32))(mixed, first, other)
     grams = call(add_kernel, "add", [VMEM, VMEM, ANY], shape((rank, width), F32), cost_estimate=small)(
         grams, arrived, partial

time: 50.5 us -> 49.9 us (0.988)
  waiting for transfers between devices: 6.55 us -> 5.01 us
  Pallas kernels: 9.71 us -> 10.9 us
    ppermute x1, waiting for transfers between devices: 1.54 us -> 0.01 us  [body(): lax.ppermute(first, 'rows', [(r, r ^ 1) for r in range(lax.axis_size('row...]
    pallas_call x1 -> x2, Pallas kernels: 4.82 us -> 6.05 us  [the longest x1 3.47 us: body(): call(load_kernel, 'load', [ANY, ANY], fast(tensor.shape, F32), [pltpu.Sem...]
  transfers between devices with their start and end apart: 6 -> 6, of which waited for: 4 -> 3; matrix products, arithmetic and copies ran while one was open for 0% -> 0% of each run, Pallas kernels for 16% -> 18%
where the time goes in v7:
time: 49.9 us; the launch traced here: 49.3 us
  starting transfers between devices  19.9 us (40%)
  blocking collectives  13.4 us (27%)
  Pallas kernels  10.9 us (22%)
  waiting for transfers between devices  5.01 us (10%)
    all_to_all x1, blocking collectives, body(): lax.all_to_all(first, axes, 0, 0, tiled=True, axis_index_groups=gather_gr...  13.4 us
    all_to_all x1, starting transfers between devices, body(): lax.all_to_all(partial.reshape(racks * pods, 1, width), ('racks', 'pods')...  6.77 us
    ppermute x1, starting transfers between devices, body(): lax.ppermute(first, 'rows', [(r, r ^ 1) for r in range(lax.axis_size('row...  6.65 us
    ppermute x3, starting transfers between devices, body(): lax.ppermute(grams, 'pods', [(p, p ^ n) for p in range(pods)])  4.79 us
    ppermute x3, waiting for transfers between devices, body(): lax.ppermute(grams, 'pods', [(p, p ^ n) for p in range(pods)])  4.68 us
    pallas_call x1, Pallas kernels, body(): call(load_kernel, 'load', [ANY, ANY], fast(tensor.shape, F32), [pltpu.Sem...  3.47 us
    pallas_call x1, Pallas kernels, body(): call(mixed_kernel, 'mixed', [VMEM] * 3, fast((slabs, pods, half, width),...  2.58 us
    pallas_call x1, Pallas kernels, body(): call(factor_kernel, 'factor', [VMEM] * len(parts), shape((rank, 3 * rank)...  2.16 us
  transfers between devices with their start and end apart: 6, of which 3 were waited for; matrix products, arithmetic and copies ran while one was open for 0% of the time, Pallas kernels for 18%

profile of v7, /device:TPU:8, one launch (start us, length us, event | category | flops | bytes accessed | tf_op | source)
XLA Modules:
  0.0 49.3 jit_solution(15712173611887243434)
XLA Ops:
  0.0 1.0 %first.1 = f32[8,128,128]{2,1,0:T(8,128)S(1)} custom-call(f32[64,256]{1,0:T(8,128)} %bitcast.6, f32[64,64]{1,0:T(8,128)} %c_ref.1), custom_call_target="tpu_custom_call" | custom-call | tf_op jit(solution)/shard_map/first/pallas_call | solution.py:208
  1.0 13.4 %all_to_all.10.after_ref.own_ref = f32[8,128,128]{2,1,0:T(8,128)S(1)} all-to-all(f32[8,128,128]{2,1,0:T(8,128)S(1)} %first.1), channel_id=1, replica_groups={{0,129,2,131,4,133,6,135},{8,137,10,139,12,141,14,143},{16,145,18,147,2..., dimensions={0} | all-to-all | bytes 1048576 | tf_op jit(solution)/shard_map/all_to_all | solution.py:215
  14.5 6.6 %collective-permute-start = (f32[8,128,128]{2,1,0:T(8,128)S(1)}, f32[8,128,128]{2,1,0:T(8,128)S(1)}, u32[]{:S(2)}, u32[]{:S(2)}) collective-permute-start(f32[8,128,128]{2,1,0:T(8,128)S(1)} %all_to_all.10.after_ref.own_ref), channel_id=1, source_target_pairs={{0,64},{64,0},{128,192},{192,128},{1,65},{65,1},{129,193},{193,129... | collective-permute-start | bytes 1572872 | tf_op jit(solution)/shard_map/ppermute | solution.py:216
  21.1 3.5 %load.1.t_ref = f32[2,2048,512]{2,1,0:T(8,128)S(1)} custom-call(f32[2,2048,512]{2,1,0:T(8,128)} %t_ref.1, f32[8,128,128]{2,1,0:T(8,128)S(1)} %all_to_all.10.after_ref.own_ref), custom_call_target="tpu_custom_call" | custom-call | bytes 8388608 | tf_op jit(solution)/shard_map/load/pallas_call | solution.py:219
  24.6 0.0 collective-permute-done.other_ref
  24.7 1.7 %collective-permute-start.1 = (f32[64,128]{1,0:T(8,128)S(1)}, f32[64,128]{1,0:T(8,128)S(1)}, u32[]{:S(2)}, u32[]{:S(2)}) collective-permute-start(f32[64,128]{1,0:T(8,128)S(1)} %grams.1.x_ref), channel_id=1, source_target_pairs={{0,129},{1,128},{2,131},{3,130},{4,133},{5,132},{6,135},{7,134},{8... | collective-permute-start | bytes 98312 | tf_op jit(solution)/shard_map/ppermute | solution.py:218
  26.3 2.6 %mixed.1.mixed_ref = f32[2,8,128,128]{3,2,1,0:T(8,128)S(1)} custom-call(f32[2,2048,512]{2,1,0:T(8,128)S(1)} %load.1.t_ref, f32[8,128,128]{2,1,0:T(8,128)S(1)} %all_to_all.10.after_ref.own_ref, f32[8,128,128]{2,1,0:T(8,128)S(1)} %collective-permute-done.other_ref), custom_call_target="tpu_custom_call" | custom-call | flops 1073741824 | bytes 8388608 | tf_op jit(solution)/shard_map/mixed/pallas_call | solution.py:227
  28.9 0.8 %partial.1.after_ref = f32[64,128]{1,0:T(8,128)} custom-call(f32[2,8,128,128]{3,2,1,0:T(8,128)S(1)} %mixed.1.mixed_ref, f32[8,128,128]{2,1,0:T(8,128)S(1)} %all_to_all.10.after_ref.own_ref, f32[8,128,128]{2,1,0:T(8,128)S(1)} %collective-permute-done.other_ref), custom_call_target="tpu_custom_call" | custom-call | tf_op jit(solution)/shard_map/partial/pallas_call | solution.py:236
  29.7 6.8 %all-to-all-start.1 = ((f32[64,1,128]{2,1,0:T(1,128)}), f32[64,1,128]{2,1,0:T(1,128)S(1)}, u32[]{:S(2)}, u32[]{:S(2)}) async-start(f32[64,1,128]{2,1,0:T(1,128)} %bitcast.2), calls=%async_computation.1 | async-start | bytes 65536 | tf_op jit(solution)/shard_map/all_to_all | solution.py:241
  36.5 0.0 collective-permute-done.1.y_ref
  36.5 1.7 %collective-permute-start.2 = (f32[64,128]{1,0:T(8,128)S(1)}, f32[64,128]{1,0:T(8,128)S(1)}, u32[]{:S(2)}, u32[]{:S(2)}) collective-permute-start(f32[64,128]{1,0:T(8,128)S(1)} %add.1.refs_0_), channel_id=1, source_target_pairs={{0,2},{1,3},{2,0},{3,1},{4,6},{5,7},{6,4},{7,5},{8,10},{9,11},{10,... | collective-permute-start | bytes 98312 | tf_op jit(solution)/shard_map/ppermute | solution.py:240
  38.2 2.7 %collective-permute-start.3 = (f32[64,128]{1,0:T(8,128)S(1)}, f32[64,128]{1,0:T(8,128)S(1)}, u32[]{:S(2)}, u32[]{:S(2)}) collective-permute-start(f32[64,128]{1,0:T(8,128)S(1)} %add.1.refs_0_), channel_id=1, source_target_pairs={{0,4},{1,5},{2,6},{3,7},{4,0},{5,1},{6,2},{7,3},{8,12},{9,13},{10,... | collective-permute-start | bytes 98312 | tf_op jit(solution)/shard_map/ppermute | solution.py:240
  40.9 0.5 collective-permute-start.4
  41.3 0.0 collective-permute-done.2.refs_1_
  41.3 2.3 %collective-permute-done.3.refs_2_ = f32[64,128]{1,0:T(8,128)S(1)} collective-permute-done((f32[64,128]{1,0:T(8,128)S(1)}, f32[64,128]{1,0:T(8,128)S(1)}, u32[]{:S(2)}, u32[]{:S(2)}) %collective-permute-start.3) | collective-permute-done | bytes 32800 | tf_op jit(solution)/shard_map/ppermute | solution.py:240
  43.6 2.4 %collective-permute-done.4.refs_3_ = f32[64,128]{1,0:T(8,128)S(1)} collective-permute-done((f32[64,128]{1,0:T(8,128)S(1)}, f32[64,128]{1,0:T(8,128)S(1)}, u32[]{:S(2)}, u32[]{:S(2)}) %collective-permute-start.4) | collective-permute-done | bytes 32800 | tf_op jit(solution)/shard_map/ppermute | solution.py:240
  46.0 2.2 %factor.1.inverse_ref = bf16[64,192]{1,0:T(8,128)(2,1)S(1)} custom-call(f32[64,128]{1,0:T(8,128)S(1)} %add.1.refs_0_, f32[64,128]{1,0:T(8,128)S(1)} %collective-permute-done.2.refs_1_, f32[64,128]{1,0:T(8,128)S(1)} %collective-permute-done.3.refs_2_, f32[64,128]{1,0:T(8,128)S(1)} %collective-permute-done.4.refs_3_), custom_call_target="tpu_custom_call" | custom-call | flops 1000000 | bytes 80000 | tf_op jit(solution)/shard_map/factor/pallas_call | solution.py:242
  48.2 0.3 all-to-all-done.1
  48.5 0.8 %last.1 = f32[2,64]{1,0:T(2,128)} custom-call(f32[64,128]{1,0:T(8,128)S(1)} %bitcast.5, bf16[64,192]{1,0:T(8,128)(2,1)S(1)} %factor.1.inverse_ref), custom_call_target="tpu_custom_call" | custom-call | tf_op jit(solution)/shard_map/last/pallas_call | solution.py:250
  (2 shorter events, 0.0 us)
Async XLA Ops:
  14.5 10.1 %collective-permute-start = (f32[8,128,128]{2,1,0:T(8,128)S(1)}, f32[8,128,128]{2,1,0:T(8,128)S(1)}, u32[]{:S(2)}, u32[]{:S(2)}) collective-permute-start(f32[8,128,128]{2,1,0:T(8,128)S(1)} %all_to_all.10.after_ref.own_ref), channel_id=1, source_target_pairs={{0,64},{64,0},{128,192},{192,128},{1,65},{65,1},{129,193},{193,129... | collective-permute-start | bytes 1572872 | tf_op jit(solution)/shard_map/ppermute | solution.py:216
  24.7 11.8 %collective-permute-start.1 = (f32[64,128]{1,0:T(8,128)S(1)}, f32[64,128]{1,0:T(8,128)S(1)}, u32[]{:S(2)}, u32[]{:S(2)}) collective-permute-start(f32[64,128]{1,0:T(8,128)S(1)} %grams.1.x_ref), channel_id=1, source_target_pairs={{0,129},{1,128},{2,131},{3,130},{4,133},{5,132},{6,135},{7,134},{8... | collective-permute-start | bytes 98312 | tf_op jit(solution)/shard_map/ppermute | solution.py:218
  29.7 18.8 %all-to-all-start.1 = ((f32[64,1,128]{2,1,0:T(1,128)}), f32[64,1,128]{2,1,0:T(1,128)S(1)}, u32[]{:S(2)}, u32[]{:S(2)}) async-start(f32[64,1,128]{2,1,0:T(1,128)} %bitcast.2), calls=%async_computation.1 | async-start | bytes 65536 | tf_op jit(solution)/shard_map/all_to_all | solution.py:241
  36.5 4.8 %collective-permute-start.2 = (f32[64,128]{1,0:T(8,128)S(1)}, f32[64,128]{1,0:T(8,128)S(1)}, u32[]{:S(2)}, u32[]{:S(2)}) collective-permute-start(f32[64,128]{1,0:T(8,128)S(1)} %add.1.refs_0_), channel_id=1, source_target_pairs={{0,2},{1,3},{2,0},{3,1},{4,6},{5,7},{6,4},{7,5},{8,10},{9,11},{10,... | collective-permute-start | bytes 98312 | tf_op jit(solution)/shard_map/ppermute | solution.py:240
  38.2 5.5 %collective-permute-start.3 = (f32[64,128]{1,0:T(8,128)S(1)}, f32[64,128]{1,0:T(8,128)S(1)}, u32[]{:S(2)}, u32[]{:S(2)}) collective-permute-start(f32[64,128]{1,0:T(8,128)S(1)} %add.1.refs_0_), channel_id=1, source_target_pairs={{0,4},{1,5},{2,6},{3,7},{4,0},{5,1},{6,2},{7,3},{8,12},{9,13},{10,... | collective-permute-start | bytes 98312 | tf_op jit(solution)/shard_map/ppermute | solution.py:240
  40.9 5.1 %collective-permute-start.4 = (f32[64,128]{1,0:T(8,128)S(1)}, f32[64,128]{1,0:T(8,128)S(1)}, u32[]{:S(2)}, u32[]{:S(2)}) collective-permute-start(f32[64,128]{1,0:T(8,128)S(1)} %add.1.refs_0_), channel_id=1, source_target_pairs={{0,6},{1,7},{2,4},{3,5},{4,2},{5,3},{6,0},{7,1},{8,14},{9,15},{10,... | collective-permute-start | bytes 98312 | tf_op jit(solution)/shard_map/ppermute | solution.py:240

commit v8 on v7

--- a/solution.py
+++ b/solution.py
@@ -132,7 +132,7 @@
 def factor_kernel(*refs):
     parts, out_ref, (grams, inverse) = refs[:-3], refs[-3], refs[-2:]
     rank = inverse.shape[0]
-    for n, part in enumerate(parts):
+    for n, part in zip((0, 2, 3, 1), parts, strict=True):
         grams[jnp.bitwise_xor(lax.axis_index("pods") // 2, n)] = part[...]
     both = grams[0]
     for n in range(1, len(parts)):
@@ -237,7 +237,8 @@
     grams = call(add_kernel, "add", [VMEM, VMEM, ANY], shape((rank, width), F32), cost_estimate=small)(
         grams, arrived, partial
     )
-    parts = [grams] + [lax.ppermute(grams, "pods", [(p, p ^ n) for p in range(pods)]) for n in range(2, pods, 2)]
+    order = (4, 6, 2)
+    parts = [grams] + [lax.ppermute(grams, "pods", [(p, p ^ n) for p in range(pods)]) for n in order]
     everyone = lax.all_to_all(partial.reshape(racks * pods, 1, width), ("racks", "pods"), 0, 0, tiled=True)
     inverse = call(
         factor_kernel,

time: 49.9 us -> 49.5 us (level)
  starting transfers between devices: 19.9 us -> 19.4 us
    all_to_all x1, waiting for transfers between devices: 0.33 us -> 1.49 us  [body(): lax.all_to_all(partial.reshape(racks * pods, 1, width), ('racks', 'pods')...]
    ppermute x3, waiting for transfers between devices: 4.68 us -> 3.97 us  [body(): lax.ppermute(grams, 'pods', [(p, p ^ n) for p in range(pods)])]
where the time goes in v8:
time: 49.5 us; the launch traced here: 49.3 us
  starting transfers between devices  19.4 us (39%)
  blocking collectives  13.4 us (27%)
  Pallas kernels  10.9 us (22%)
  waiting for transfers between devices  5.47 us (11%)
    all_to_all x1, blocking collectives, body(): lax.all_to_all(first, axes, 0, 0, tiled=True, axis_index_groups=gather_gr...  13.4 us
    all_to_all x1, starting transfers between devices, body(): lax.all_to_all(partial.reshape(racks * pods, 1, width), ('racks', 'pods')...  6.77 us
    ppermute x1, starting transfers between devices, body(): lax.ppermute(first, 'rows', [(r, r ^ 1) for r in range(lax.axis_size('row...  6.65 us
    ppermute x3, starting transfers between devices, body(): lax.ppermute(grams, 'pods', [(p, p ^ n) for p in range(pods)])  4.33 us
    ppermute x3, waiting for transfers between devices, body(): lax.ppermute(grams, 'pods', [(p, p ^ n) for p in range(pods)])  3.97 us
    pallas_call x1, Pallas kernels, body(): call(load_kernel, 'load', [ANY, ANY], fast(tensor.shape, F32), [pltpu.Sem...  3.47 us
    pallas_call x1, Pallas kernels, body(): call(mixed_kernel, 'mixed', [VMEM] * 3, fast((slabs, pods, half, width),...  2.58 us
    pallas_call x1, Pallas kernels, body(): call(factor_kernel, 'factor', [VMEM] * len(parts), shape((rank, 3 * rank)...  2.16 us
  transfers between devices with their start and end apart: 6, of which 3 were waited for; matrix products, arithmetic and copies ran while one was open for 0% of the time, Pallas kernels for 18%

profile of v8, /device:TPU:8, one launch (start us, length us, event | category | flops | bytes accessed | tf_op | source)
XLA Modules:
  0.0 49.3 jit_solution(941899679518089524)
XLA Ops:
  0.0 1.0 %first.1 = f32[8,128,128]{2,1,0:T(8,128)S(1)} custom-call(f32[64,256]{1,0:T(8,128)} %bitcast.6, f32[64,64]{1,0:T(8,128)} %c_ref.1), custom_call_target="tpu_custom_call" | custom-call | tf_op jit(solution)/shard_map/first/pallas_call | solution.py:208
  1.0 13.4 %all_to_all.10.after_ref.own_ref = f32[8,128,128]{2,1,0:T(8,128)S(1)} all-to-all(f32[8,128,128]{2,1,0:T(8,128)S(1)} %first.1), channel_id=1, replica_groups={{0,129,2,131,4,133,6,135},{8,137,10,139,12,141,14,143},{16,145,18,147,2..., dimensions={0} | all-to-all | bytes 1048576 | tf_op jit(solution)/shard_map/all_to_all | solution.py:215
  14.5 6.6 %collective-permute-start = (f32[8,128,128]{2,1,0:T(8,128)S(1)}, f32[8,128,128]{2,1,0:T(8,128)S(1)}, u32[]{:S(2)}, u32[]{:S(2)}) collective-permute-start(f32[8,128,128]{2,1,0:T(8,128)S(1)} %all_to_all.10.after_ref.own_ref), channel_id=1, source_target_pairs={{0,64},{64,0},{128,192},{192,128},{1,65},{65,1},{129,193},{193,129... | collective-permute-start | bytes 1572872 | tf_op jit(solution)/shard_map/ppermute | solution.py:216
  21.1 3.5 %load.1.t_ref = f32[2,2048,512]{2,1,0:T(8,128)S(1)} custom-call(f32[2,2048,512]{2,1,0:T(8,128)} %t_ref.1, f32[8,128,128]{2,1,0:T(8,128)S(1)} %all_to_all.10.after_ref.own_ref), custom_call_target="tpu_custom_call" | custom-call | bytes 8388608 | tf_op jit(solution)/shard_map/load/pallas_call | solution.py:219
  24.6 0.0 collective-permute-done.other_ref
  24.7 1.7 %collective-permute-start.1 = (f32[64,128]{1,0:T(8,128)S(1)}, f32[64,128]{1,0:T(8,128)S(1)}, u32[]{:S(2)}, u32[]{:S(2)}) collective-permute-start(f32[64,128]{1,0:T(8,128)S(1)} %grams.1.x_ref), channel_id=1, source_target_pairs={{0,129},{1,128},{2,131},{3,130},{4,133},{5,132},{6,135},{7,134},{8... | collective-permute-start | bytes 98312 | tf_op jit(solution)/shard_map/ppermute | solution.py:218
  26.3 2.6 %mixed.1.mixed_ref = f32[2,8,128,128]{3,2,1,0:T(8,128)S(1)} custom-call(f32[2,2048,512]{2,1,0:T(8,128)S(1)} %load.1.t_ref, f32[8,128,128]{2,1,0:T(8,128)S(1)} %all_to_all.10.after_ref.own_ref, f32[8,128,128]{2,1,0:T(8,128)S(1)} %collective-permute-done.other_ref), custom_call_target="tpu_custom_call" | custom-call | flops 1073741824 | bytes 8388608 | tf_op jit(solution)/shard_map/mixed/pallas_call | solution.py:227
  28.9 0.8 %partial.1.after_ref = f32[64,128]{1,0:T(8,128)} custom-call(f32[2,8,128,128]{3,2,1,0:T(8,128)S(1)} %mixed.1.mixed_ref, f32[8,128,128]{2,1,0:T(8,128)S(1)} %all_to_all.10.after_ref.own_ref, f32[8,128,128]{2,1,0:T(8,128)S(1)} %collective-permute-done.other_ref), custom_call_target="tpu_custom_call" | custom-call | tf_op jit(solution)/shard_map/partial/pallas_call | solution.py:236
  29.7 6.8 %all-to-all-start.1 = ((f32[64,1,128]{2,1,0:T(1,128)}), f32[64,1,128]{2,1,0:T(1,128)S(1)}, u32[]{:S(2)}, u32[]{:S(2)}) async-start(f32[64,1,128]{2,1,0:T(1,128)} %bitcast.2), calls=%async_computation.1 | async-start | bytes 65536 | tf_op jit(solution)/shard_map/all_to_all | solution.py:242
  36.5 0.0 collective-permute-done.1.y_ref
  36.5 3.2 %collective-permute-start.2 = (f32[64,128]{1,0:T(8,128)S(1)}, f32[64,128]{1,0:T(8,128)S(1)}, u32[]{:S(2)}, u32[]{:S(2)}) collective-permute-start(f32[64,128]{1,0:T(8,128)S(1)} %add.1.refs_0_), channel_id=1, source_target_pairs={{0,4},{1,5},{2,6},{3,7},{4,0},{5,1},{6,2},{7,3},{8,12},{9,13},{10,... | collective-permute-start | bytes 98312 | tf_op jit(solution)/shard_map/ppermute | solution.py:241
  39.7 1.2 %collective-permute-start.3 = (f32[64,128]{1,0:T(8,128)S(1)}, f32[64,128]{1,0:T(8,128)S(1)}, u32[]{:S(2)}, u32[]{:S(2)}) collective-permute-start(f32[64,128]{1,0:T(8,128)S(1)} %add.1.refs_0_), channel_id=1, source_target_pairs={{0,6},{1,7},{2,4},{3,5},{4,2},{5,3},{6,0},{7,1},{8,14},{9,15},{10,... | collective-permute-start | bytes 98312 | tf_op jit(solution)/shard_map/ppermute | solution.py:241
  40.9 0.0 collective-permute-start.4
  40.9 1.2 %collective-permute-done.2.refs_1_ = f32[64,128]{1,0:T(8,128)S(1)} collective-permute-done((f32[64,128]{1,0:T(8,128)S(1)}, f32[64,128]{1,0:T(8,128)S(1)}, u32[]{:S(2)}, u32[]{:S(2)}) %collective-permute-start.2) | collective-permute-done | bytes 32800 | tf_op jit(solution)/shard_map/ppermute | solution.py:241
  42.1 2.8 %collective-permute-done.3.refs_2_ = f32[64,128]{1,0:T(8,128)S(1)} collective-permute-done((f32[64,128]{1,0:T(8,128)S(1)}, f32[64,128]{1,0:T(8,128)S(1)}, u32[]{:S(2)}, u32[]{:S(2)}) %collective-permute-start.3) | collective-permute-done | bytes 32800 | tf_op jit(solution)/shard_map/ppermute | solution.py:241
  44.8 0.0 collective-permute-done.4.refs_3_
  44.8 2.2 %factor.1.inverse_ref = bf16[64,192]{1,0:T(8,128)(2,1)S(1)} custom-call(f32[64,128]{1,0:T(8,128)S(1)} %add.1.refs_0_, f32[64,128]{1,0:T(8,128)S(1)} %collective-permute-done.2.refs_1_, f32[64,128]{1,0:T(8,128)S(1)} %collective-permute-done.3.refs_2_, f32[64,128]{1,0:T(8,128)S(1)} %collective-permute-done.4.refs_3_), custom_call_target="tpu_custom_call" | custom-call | flops 1000000 | bytes 80000 | tf_op jit(solution)/shard_map/factor/pallas_call | solution.py:243
  47.0 1.5 %all-to-all-done.1 = f32[64,1,128]{2,1,0:T(1,128)S(1)} async-done(((f32[64,1,128]{2,1,0:T(1,128)}), f32[64,1,128]{2,1,0:T(1,128)S(1)}, u32[]{:S(2)}, u32[]{:S(2)}) %all-to-all-start.1) | async-done | bytes 32800 | tf_op jit(solution)/shard_map/all_to_all | solution.py:242
  48.5 0.8 %last.1 = f32[2,64]{1,0:T(2,128)} custom-call(f32[64,128]{1,0:T(8,128)S(1)} %bitcast.5, bf16[64,192]{1,0:T(8,128)(2,1)S(1)} %factor.1.inverse_ref), custom_call_target="tpu_custom_call" | custom-call | tf_op jit(solution)/shard_map/last/pallas_call | solution.py:251
  (2 shorter events, 0.0 us)
Async XLA Ops:
  14.5 10.1 %collective-permute-start = (f32[8,128,128]{2,1,0:T(8,128)S(1)}, f32[8,128,128]{2,1,0:T(8,128)S(1)}, u32[]{:S(2)}, u32[]{:S(2)}) collective-permute-start(f32[8,128,128]{2,1,0:T(8,128)S(1)} %all_to_all.10.after_ref.own_ref), channel_id=1, source_target_pairs={{0,64},{64,0},{128,192},{192,128},{1,65},{65,1},{129,193},{193,129... | collective-permute-start | bytes 1572872 | tf_op jit(solution)/shard_map/ppermute | solution.py:216
  24.7 11.8 %collective-permute-start.1 = (f32[64,128]{1,0:T(8,128)S(1)}, f32[64,128]{1,0:T(8,128)S(1)}, u32[]{:S(2)}, u32[]{:S(2)}) collective-permute-start(f32[64,128]{1,0:T(8,128)S(1)} %grams.1.x_ref), channel_id=1, source_target_pairs={{0,129},{1,128},{2,131},{3,130},{4,133},{5,132},{6,135},{7,134},{8... | collective-permute-start | bytes 98312 | tf_op jit(solution)/shard_map/ppermute | solution.py:218
  29.7 18.8 %all-to-all-start.1 = ((f32[64,1,128]{2,1,0:T(1,128)}), f32[64,1,128]{2,1,0:T(1,128)S(1)}, u32[]{:S(2)}, u32[]{:S(2)}) async-start(f32[64,1,128]{2,1,0:T(1,128)} %bitcast.2), calls=%async_computation.1 | async-start | bytes 65536 | tf_op jit(solution)/shard_map/all_to_all | solution.py:242
  36.5 5.5 %collective-permute-start.2 = (f32[64,128]{1,0:T(8,128)S(1)}, f32[64,128]{1,0:T(8,128)S(1)}, u32[]{:S(2)}, u32[]{:S(2)}) collective-permute-start(f32[64,128]{1,0:T(8,128)S(1)} %add.1.refs_0_), channel_id=1, source_target_pairs={{0,4},{1,5},{2,6},{3,7},{4,0},{5,1},{6,2},{7,3},{8,12},{9,13},{10,... | collective-permute-start | bytes 98312 | tf_op jit(solution)/shard_map/ppermute | solution.py:241
  39.7 5.1 %collective-permute-start.3 = (f32[64,128]{1,0:T(8,128)S(1)}, f32[64,128]{1,0:T(8,128)S(1)}, u32[]{:S(2)}, u32[]{:S(2)}) collective-permute-start(f32[64,128]{1,0:T(8,128)S(1)} %add.1.refs_0_), channel_id=1, source_target_pairs={{0,6},{1,7},{2,4},{3,5},{4,2},{5,3},{6,0},{7,1},{8,14},{9,15},{10,... | collective-permute-start | bytes 98312 | tf_op jit(solution)/shard_map/ppermute | solution.py:241
  40.9 4.0 %collective-permute-start.4 = (f32[64,128]{1,0:T(8,128)S(1)}, f32[64,128]{1,0:T(8,128)S(1)}, u32[]{:S(2)}, u32[]{:S(2)}) collective-permute-start(f32[64,128]{1,0:T(8,128)S(1)} %add.1.refs_0_), channel_id=1, source_target_pairs={{0,2},{1,3},{2,0},{3,1},{4,6},{5,7},{6,4},{7,5},{8,10},{9,11},{10,... | collective-permute-start | bytes 98312 | tf_op jit(solution)/shard_map/ppermute | solution.py:241
